TPU v7x, 512 devices: a whole 4x8x8 slice. The times are simulated.
512 devices in a mesh: sec: 2 (over core), frm: 32 (over y, x), clip: 8 (over z).
Axes of the slice: x: 4, y: 8, z: 8, core: 2. Of those that a mesh axis runs over, the one named last changes fastest.
Arguments:
- hidden: bfloat16 [8, 128, 64, 5120], P('clip', 'frm', None, 'sec'), may hold values from -150 to 150
- modulation: float32 [8, 2, 5120], P('clip', None, 'sec'), may hold values from -3 to 3
- head_w: bfloat16 [5120, 64], P('sec'), may hold values from -2 to 2
- clip_ids: int32 [8, 128], P('clip'), may hold values from 0 to 6, never falling along the last dimension, each value on 1 to 21 neighbouring positions
- w_in: bfloat16 [3, 16, 384], replicated, may hold values from -0.875 to 0.875
- gain_one: float32 [384], replicated, may hold values from 0.5 to 1.5
- w_one: bfloat16 [3, 384, 384], replicated, may hold values from -0.1875 to 0.1875
- w_up: bfloat16 [3, 384, 192], replicated, may hold values from -0.1875 to 0.1875
- gain_two: float32 [96], replicated, may hold values from 0.5 to 1.5
- w_two: bfloat16 [3, 96, 96], replicated, may hold values from -0.375 to 0.375
- reward_grad: bfloat16 [8, 256, 256, 96], P('clip', 'frm', 'sec'), may hold values from -6 to 6
Outputs:
- decoded: bfloat16 [8, 256, 256, 96], P('clip', 'frm', 'sec')
- hidden_grad: bfloat16 [8, 128, 64, 5120], P('clip', 'frm', None, 'sec')
Inputs may be any that keep to these rules, and one draw needn't show every extreme that they name: `clip_ids`: ids never fall along a row; each clip spans 1 to min(21, 128) frames, and one spans exactly that many.
All inputs are finite; a program needn't handle non-finite values.
Results may differ from a plain program's by a relative error of at most 0.023.
Values may be sent and summed in bfloat16 or wider, within the bound.
A program may use at most 64 MiB of HBM per device.

v0:
```python
import jax
import jax.numpy as jnp
from jax import lax
from jax.sharding import PartitionSpec as P

DD = 5120


def shifted_2(block, axis, distance):
    devices = range(lax.axis_size(axis))
    route = [(i - distance, i) for i in devices if i - distance in devices]
    return lax.ppermute(block, axis, route)


def seg_lookup(seg_row, frame_ids):
    total = seg_row.shape[0]
    hits = frame_ids[:, None] == jnp.arange(total, dtype=jnp.int32)[None, :]
    return jnp.sum(jnp.where(hits, seg_row[None, :], 0), axis=1)


def frame_masks(seg_row, first, count):
    total = seg_row.shape[0]
    frame_ids = first + jnp.arange(count, dtype=jnp.int32)
    own_ids = seg_lookup(seg_row, frame_ids)
    inside = (frame_ids >= 0) & (frame_ids < total)
    stacked = []
    for offset in range(3):
        earlier = frame_ids - offset
        same = inside & (earlier >= 0) & (seg_lookup(seg_row, earlier) == own_ids)
        stacked.append(same.astype(jnp.float32))
    return jnp.stack(stacked)


def causal(extended, weight, mask_rows):
    length = extended.shape[0] - 2
    pixels = extended.shape[1]
    summed = jnp.zeros((length * pixels, weight.shape[2]), jnp.float32)
    for offset in range(3):
        shifted = extended[2 - offset : 2 - offset + length] * mask_rows[offset][
            :, None, None
        ].astype(extended.dtype)
        summed = summed + jnp.dot(
            shifted.reshape(length * pixels, -1), weight[offset], preferred_element_type=jnp.float32
        )
    return summed.reshape(length, pixels, -1)


def causal_back(extended, weight, mask_rows):
    length = extended.shape[0] - 2
    pixels = extended.shape[1]
    summed = jnp.zeros((length * pixels, weight.shape[1]), jnp.float32)
    for offset in range(3):
        picked = mask_rows[offset][offset : offset + length]
        shifted = extended[offset : offset + length] * picked[:, None, None].astype(extended.dtype)
        summed = summed + jnp.dot(
            shifted.reshape(length * pixels, -1),
            weight[offset].T,
            preferred_element_type=jnp.float32,
        )
    return summed.reshape(length, pixels, -1)


def rms_silu(values, gain):
    inverse = lax.rsqrt(jnp.mean(values * values, axis=-1, keepdims=True) + 1e-06)
    normed = values * inverse * gain
    return (normed * jax.nn.sigmoid(normed)).astype(jnp.bfloat16)


def rms_silu_back(grads, values, gain):
    inverse = lax.rsqrt(jnp.mean(values * values, axis=-1, keepdims=True) + 1e-06)
    normed = values * inverse * gain
    sigmoid_part = jax.nn.sigmoid(normed)
    weighted = grads * sigmoid_part * (1.0 + normed * (1.0 - sigmoid_part)) * gain
    return inverse * weighted - values * inverse * inverse * inverse * jnp.mean(
        weighted * values, axis=-1, keepdims=True
    )


def widen_kernel(w_in):
    identity = jnp.eye(4, dtype=w_in.dtype)
    return jnp.stack([jnp.kron(identity, w_in[offset]) for offset in range(3)])


def decode_forward(latent, first, seg_row, seg_two, weights, before):
    w_big, gain_one, w_one, w_up, gain_two, w_two = weights
    frames = latent.shape[0]
    tokens = latent.shape[1]
    lat_masks = frame_masks(seg_row, first, frames)
    out_masks = frame_masks(seg_two, 2 * first, 2 * frames)
    lat_ext = jnp.concatenate([before(latent, 0), latent])
    base = causal(lat_ext, w_big, lat_masks).reshape(frames, 4 * tokens, -1).astype(jnp.bfloat16)
    act_one = rms_silu(base.astype(jnp.float32), gain_one)
    trunk = base.astype(jnp.float32) + causal(
        jnp.concatenate([before(act_one, 1), act_one]), w_one, lat_masks
    )
    trunk = trunk.astype(jnp.bfloat16)
    raised = causal(jnp.concatenate([before(trunk, 2), trunk]), w_up, lat_masks)
    pixels = raised.shape[1]
    upsampled = (
        raised.reshape(frames, pixels, 2, -1).transpose(0, 2, 1, 3).reshape(2 * frames, pixels, -1)
    )
    upsampled = upsampled.astype(jnp.bfloat16)
    act_two = rms_silu(upsampled.astype(jnp.float32), gain_two)
    decoded = upsampled.astype(jnp.float32) + causal(
        jnp.concatenate([before(act_two, 3), act_two]), w_two, out_masks
    )
    return (base, upsampled, decoded.astype(jnp.bfloat16))


def decode_backward(reward_grad, base, upsampled, first, seg_row, seg_two, weights, after):
    w_big, gain_one, w_one, w_up, gain_two, w_two = weights
    frames = base.shape[0]
    tokens = base.shape[1] // 4
    lat_masks = frame_masks(seg_row, first, frames + 2)
    out_masks = frame_masks(seg_two, 2 * first, 2 * frames + 2)
    second_grad = causal_back(
        jnp.concatenate([reward_grad, after(reward_grad, 2, 0)]), w_two, out_masks
    )
    up_grad = reward_grad.astype(jnp.float32) + rms_silu_back(
        second_grad, upsampled.astype(jnp.float32), gain_two
    )
    up_grad = up_grad.astype(jnp.bfloat16)
    up_ext = jnp.concatenate([up_grad, after(up_grad, 4, 1)])
    pixels = up_ext.shape[1]
    folded = (
        up_ext.reshape(frames + 2, 2, pixels, -1)
        .transpose(0, 2, 1, 3)
        .reshape(frames + 2, pixels, -1)
    )
    trunk_grad = causal_back(folded, w_up, lat_masks).astype(jnp.bfloat16)
    first_grad = causal_back(
        jnp.concatenate([trunk_grad, after(trunk_grad, 2, 2)]), w_one, lat_masks
    )
    base_grad = trunk_grad.astype(jnp.float32) + rms_silu_back(
        first_grad, base.astype(jnp.float32), gain_one
    )
    base_grad = base_grad.astype(jnp.bfloat16)
    base_ext = jnp.concatenate([base_grad, after(base_grad, 2, 3)])
    latent_grad = causal_back(base_ext.reshape(frames + 2, tokens, -1), w_big, lat_masks)
    return latent_grad.astype(jnp.bfloat16)


def prior_frames(values, phase_number):
    if phase_number == 0:
        return shifted_2(values[-2:], "frm", 1)
    if phase_number == 1:
        return shifted_2(values[-2:], "frm", 1)
    if phase_number == 2:
        return shifted_2(values[-2:], "frm", 1)
    return shifted_2(values[-2:], "frm", 1)


def later_frames(values, count, phase_number):
    if phase_number == 0:
        return shifted_2(values[:count], "frm", -1)
    if phase_number == 1:
        return shifted_2(values[:count], "frm", -1)
    if phase_number == 2:
        return shifted_2(values[:count], "frm", -1)
    return shifted_2(values[:count], "frm", -1)


def body(
    hidden, modulation, head_w, clip_ids, w_in, gain_one, w_one, w_up, gain_two, w_two, reward_grad
):
    weights = (widen_kernel(w_in), gain_one, w_one, w_up, gain_two, w_two)
    frames = hidden.shape[1]
    tokens = hidden.shape[2]
    features = hidden.shape[3]
    shift_row = modulation[0, 0]
    scale_row = modulation[0, 1]
    values = hidden[0].astype(jnp.float32)
    row_sum, row_squares = lax.psum(
        (jnp.sum(values, axis=-1, keepdims=True), jnp.sum(values * values, axis=-1, keepdims=True)),
        "sec",
    )
    mean = row_sum / DD
    inverse = lax.rsqrt(row_squares / DD - mean * mean + 1e-06)
    normed = (values - mean) * inverse
    modulated = (normed * (1.0 + scale_row) + shift_row).astype(jnp.bfloat16)
    partial_value = jnp.dot(
        modulated.reshape(-1, features), head_w, preferred_element_type=jnp.float32
    )
    partial_value = partial_value.reshape(frames, tokens, -1)
    latent = lax.psum_scatter(
        partial_value.astype(jnp.bfloat16), "sec", scatter_dimension=1, tiled=True
    )
    seg_row = clip_ids[0]
    seg_two = jnp.repeat(seg_row, 2)
    first = lax.axis_index("frm") * frames
    base, upsampled, decoded = decode_forward(
        latent, first, seg_row, seg_two, weights, prior_frames
    )
    latent_grad = decode_backward(
        reward_grad[0], base, upsampled, first, seg_row, seg_two, weights, later_frames
    )
    piece = lax.all_gather(latent_grad, "sec", axis=1, tiled=True)
    rows = piece.shape[1]
    product = jnp.dot(
        piece.reshape(-1, piece.shape[2]), head_w.T, preferred_element_type=jnp.float32
    )
    normed_grad = product.reshape(frames, rows, features) * (1.0 + scale_row)
    first_sum, second_sum = lax.psum(
        (
            jnp.sum(normed_grad, axis=-1, keepdims=True),
            jnp.sum(normed_grad * normed, axis=-1, keepdims=True),
        ),
        "sec",
    )
    token_grad = inverse * (normed_grad - first_sum / DD - normed * (second_sum / DD))
    count = float(
        frames
        * tokens
        * features
        * lax.axis_size("sec")
        * lax.axis_size("frm")
        * lax.axis_size("clip")
    )
    total = lax.psum(jnp.sum(token_grad * token_grad), ("sec", "frm", "clip"))
    hidden_grad = (token_grad * lax.rsqrt(total / count + 1e-06)).astype(jnp.bfloat16)
    return (decoded[None], hidden_grad[None])


def solution(mesh):
    in_specs = (
        P("clip", "frm", None, "sec"),
        P("clip", None, "sec"),
        P("sec", None),
        P("clip", None),
        P(),
        P(),
        P(),
        P(),
        P(),
        P(),
        P("clip", "frm", "sec", None),
    )
    out_specs = (P("clip", "frm", "sec", None), P("clip", "frm", None, "sec"))
    return jax.shard_map(body, mesh=mesh, in_specs=in_specs, out_specs=out_specs, check_vma=False)
```

profile of v0, /device:TPU:1, one launch (start us, length us, event | category | flops | bytes accessed | tf_op | source)
XLA Modules:
  0.0 269.9 jit_solution(17541888737887437047)
XLA Ops:
  7.2 1.8 fusion.11
  9.0 1.6 convert_reduce_fusion
  10.7 9.0 %all-reduce.1 = (f32[4,64,1]{1,0,2:T(4,128)S(1)}, f32[4,64,1]{1,0,2:T(4,128)S(1)}) all-reduce(f32[4,64,1]{1,0,2:T(4,128)S(1)} %bitcast.308, f32[4,64,1]{1,0,2:T(4,128)S(1)} %bitcast.309), channel_id=1, replica_groups=mesh['sec'=2,'frm'=32,'clip'=8] {'sec'}, use_global_device_ids=true, to_apply=%region_3.4 | all-reduce | flops 512 | bytes 4096 | tf_op jit(solution)/shard_map/psum | solution.py:173
  19.8 1.3 fusion.21
  21.8 1.3 collective-permute-start.4
  35.6 1.7 reduce-scatter.2.cloned.1.call-done
  38.0 2.2 collective-permute-start
  42.1 1.2 fusion.145
  45.6 1.0 multiply_convert_fusion.1
  46.7 1.1 reshape.562
  47.8 1.6 slice.237
  49.4 4.2 %collective-permute-start.1 = (bf16[2,128,384]{2,1,0:T(8,128)(2,1)}, bf16[2,128,384]{2,1,0:T(8,128)(2,1)}, u32[]{:S(2)}, u32[]{:S(2)}) collective-permute-start(bf16[2,128,384]{2,1,0:T(8,128)(2,1)} %slice.237), channel_id=1, source_target_pairs={{0,8},{8,16},{16,24},{24,32},{32,40},{40,48},{48,56},{56,64},{64,7... | collective-permute-start | bytes 589832 | tf_op jit(solution)/shard_map/ppermute | solution.py:12
  53.9 1.7 fusion.55
  55.6 2.0 mul.718
  58.6 2.2 mul.787
  60.8 1.5 fusion.64
  62.4 1.3 fusion.49
  64.7 2.3 collective-permute-start.2
  67.4 2.2 collective-permute-done.2
  70.1 1.0 fusion.20
  71.1 1.9 reshape.569
  74.0 1.8 copy.122
  75.8 1.2 fusion.102
  77.9 1.7 mul.743
  79.6 2.0 copy.63
  81.6 2.1 reshape.566
  83.7 1.6 multiply_reduce_fusion.3
  85.7 3.8 %collective-permute-start.3 = (bf16[2,128,96]{1,2,0:T(8,128)(2,1)S(1)}, bf16[2,128,96]{1,2,0:T(8,128)(2,1)S(1)}, u32[]{:S(2)}, u32[]{:S(2)}) collective-permute-start(bf16[2,128,96]{1,2,0:T(8,128)(2,1)S(1)} %slice.243), channel_id=1, source_target_pairs={{0,8},{8,16},{16,24},{24,32},{32,40},{40,48},{48,56},{56,64},{64,7... | collective-permute-start | bytes 147464 | tf_op jit(solution)/shard_map/ppermute | solution.py:12
  89.8 1.5 collective-permute-start.5
  92.8 3.2 %collective-permute-done.5 = bf16[4,128,96]{1,2,0:T(8,128)(2,1)S(1)} collective-permute-done((bf16[4,128,96]{1,2,0:T(8,128)(2,1)S(1)}, bf16[4,128,96]{1,2,0:T(8,128)(2,1)S(1)}, u32[]{:S(2)}, u32[]{:S(2)}) %collective-permute-start.5) | collective-permute-done | bytes 98336 | tf_op jit(solution)/shard_map/ppermute | solution.py:12
  98.5 2.1 reshape.567
  100.6 1.4 collective-permute-start.6
  102.0 1.5 fusion.53
  103.5 4.0 %collective-permute-done.6 = bf16[2,128,384]{2,1,0:T(8,128)(2,1)S(1)} collective-permute-done((bf16[2,128,384]{2,1,0:T(8,128)(2,1)S(1)}, bf16[2,128,384]{2,1,0:T(8,128)(2,1)S(1)}, u32[]{:S(2)}, u32[]{:S(2)}) %collective-permute-start.6) | collective-permute-done | bytes 196640 | tf_op jit(solution)/shard_map/ppermute | solution.py:12
  107.6 1.2 fusion.47
  109.2 1.5 multiply_reduce_fusion.1
  110.7 2.1 reshape.560
  112.8 1.9 add_convert_fusion
  115.5 1.3 collective-permute-start.7
  118.0 2.9 %fusion.51 = f32[128,64]{0,1:T(8,128)S(1)} fusion(bf16[64,1536]{1,0:T(8,128)(2,1)S(1)} %bitcast.299, bf16[128,1536]{1,0:T(8,128)(2,1)} %mul.819, f32[128,1536]{1,0:T(8,128)} %reshape.567, f32[128,1536]{1,0:T(8,128)} %mul.816, f32[128,1536]{1,0:T(8,128)} %mul.787, f32[128,1536]{1,0:T(8,128)} %mul.797, f32[128,1536]{1,0:T(8,128)} %reshape.560, ...), kind=kOutput, calls=%fused_computation.93 | convolution fusion | flops 28901376 | bytes 5341184 | tf_op jit(solution)/shard_map/dot_general | solution.py:55
  120.9 2.5 collective-permute-done.7
  123.4 1.2 fusion.46
  125.8 6.7 %all_gather.3 = bf16[4,64,64]{2,1,0:T(8,128)(2,1)S(1)} all-gather(bf16[4,32,64]{2,1,0:T(8,128)(2,1)S(1)} %bitcast.305), channel_id=1, replica_groups=mesh['sec'=2,'frm'=32,'clip'=8] {'sec'}, dimensions={1}, use_global_device_ids=true | all-gather | bytes 49152 | tf_op jit(solution)/shard_map/all_gather | solution.py:197
  132.4 2.2 fusion.144
  134.7 2.6 all-reduce
  137.3 3.7 %multiply_reduce_fusion = f32[]{:T(128)} fusion(f32[4,64]{1,0:T(4,128)S(1)} %multiply_bitcast_fusion.1, f32[4,64]{1,0:T(4,128)S(1)} %copy-done.27, bf16[1,4,64,2560]{3,2,1,0:T(8,128)(2,1)S(1)} %copy-done.1, f32[4,64,2560]{2,1,0:T(8,128)} %get-tuple-element.67, f32[4,64]{1,0:T(4,128)S(1)} %multiply_bitcast_fusion.2, f32[4,64]{1,0:T(4,128)S(1)} %copy-done.29), kind=kLoop, calls=%fused_computation.16 | loop fusion | flops 5898239 | bytes 3936260 | tf_op jit(solution)/shard_map/reduce_sum | solution.py:219
  141.7 116.9 %psum.39 = f32[]{:T(128)} all-reduce(f32[]{:T(128)} %multiply_reduce_fusion), channel_id=1, replica_groups=mesh['sec'=2,'frm'=32,'clip'=8] {'sec','frm','clip'}, use_global_device_ids=true, to_apply=%region_26.27 | all-reduce | flops 1 | bytes 8 | tf_op jit(solution)/shard_map/psum | solution.py:219
  259.3 3.7 %fusion.14 = bf16[1,4,64,2560]{3,2,1,0:T(8,128)(2,1)} fusion(f32[]{:T(128)S(6)} %rsqrt.47, f32[4,64]{1,0:T(4,128)S(1)} %multiply_bitcast_fusion.1, f32[4,64]{1,0:T(4,128)S(1)} %copy-done.27, bf16[1,4,64,2560]{3,2,1,0:T(8,128)(2,1)S(1)} %copy-done.1, f32[4,64,2560]{2,1,0:T(8,128)} %get-tuple-element.67, f32[4,64]{1,0:T(4,128)S(1)} %multiply_bitcast_fusion.2, ...), kind=kLoop, calls=%fused_computation.21 | loop fusion | flops 5898240 | bytes 5246980 | tf_op jit(solution)/shard_map/broadcast_in_dim | solution.py:221
  (210 shorter events, 31.6 us)
Async XLA Ops:
  7.2 12.6 %copy-start = (bf16[2560,64]{0,1:T(8,128)(2,1)S(1)}, bf16[2560,64]{0,1:T(8,128)(2,1)}, u32[]{:S(2)}) copy-start(bf16[2560,64]{0,1:T(8,128)(2,1)} %param.13) | copy-start | bytes 983044
  7.2 12.6 %copy-start.1 = (bf16[1,4,64,2560]{3,2,1,0:T(8,128)(2,1)S(1)}, bf16[1,4,64,2560]{3,2,1,0:T(8,128)(2,1)}, u32[]{:S(2)}) copy-start(bf16[1,4,64,2560]{3,2,1,0:T(8,128)(2,1)} %param.11) | copy-start | bytes 3932164
  7.2 30.1 %reduce-scatter.2.cloned.1.call-start = ((), (), s32[]{:S(2)}) async-start(), calls=%async_computation.1 | async-start | bytes 98304 | tf_op jit(solution)/shard_map/reduce_scatter | solution.py:185
  9.0 12.1 %copy-start.11 = (bf16[1,8,128,96]{2,3,1,0:T(8,128)(2,1)S(1)}, bf16[1,8,128,96]{2,3,1,0:T(8,128)(2,1)}, u32[]{:S(2)}) copy-start(bf16[1,8,128,96]{2,3,1,0:T(8,128)(2,1)} %param.21) | copy-start | bytes 589828
  9.0 14.2 %copy-start.37 = (s32[1,128]{1,0:T(1,128)S(1)}, s32[1,128]{1,0:T(1,128)}, u32[]{:S(2)}) copy-start(s32[1,128]{1,0:T(1,128)} %param.14) | copy-start | bytes 1540
  9.0 17.7 %copy-start.22 = (bf16[3,16,384]{2,1,0:T(8,128)(2,1)S(1)}, bf16[3,16,384]{2,1,0:T(8,128)(2,1)}, u32[]{:S(2)}) copy-start(bf16[3,16,384]{2,1,0:T(8,128)(2,1)} %param.15) | copy-start | bytes 110596
  10.7 10.4 %copy-start.30 = (f32[2560]{0:T(1024)}, f32[2560]{0:T(1024)S(1)}, u32[]{:S(2)}) copy-start(f32[2560]{0:T(1024)S(1)} %get-tuple-element.4) | copy-start | bytes 30724
  19.7 8.8 %copy-start.26 = (f32[4,64]{1,0:T(4,128)}, f32[4,64]{1,0:T(4,128)S(1)}, u32[]{:S(2)}) copy-start(f32[4,64]{1,0:T(4,128)S(1)} %get-tuple-element.50) | copy-start | bytes 3076
  19.8 8.8 %copy-start.21 = (bf16[3,96,96]{2,1,0:T(8,128)(2,1)S(1)}, bf16[3,96,96]{2,1,0:T(8,128)(2,1)}, u32[]{:S(2)}) copy-start(bf16[3,96,96]{2,1,0:T(8,128)(2,1)} %param.20) | copy-start | bytes 165892
  19.8 11.4 %copy-start.24 = (f32[384]{0:T(512)S(1)}, f32[384]{0:T(512)}, u32[]{:S(2)}) copy-start(f32[384]{0:T(512)} %param.16) | copy-start | bytes 4612
  21.8 13.0 %collective-permute-start.4 = (bf16[2,128,96]{1,2,0:T(8,128)(2,1)}, bf16[2,128,96]{1,2,0:T(8,128)(2,1)S(1)}, u32[]{:S(2)}, u32[]{:S(2)}) collective-permute-start(bf16[2,128,96]{1,2,0:T(8,128)(2,1)} %slice_bitcast_fusion), channel_id=1, source_target_pairs={{8,0},{16,8},{24,16},{32,24},{40,32},{48,40},{56,48},{64,56},{72,6... | collective-permute-start | bytes 147464 | tf_op jit(solution)/shard_map/ppermute | solution.py:12
  23.2 9.7 %copy-start.38 = (bf16[4]{0:T(256)(128)(2,1)}, bf16[4]{0:T(256)(128)(2,1)S(1)}, u32[]{:S(2)}) copy-start(bf16[4]{0:T(256)(128)(2,1)S(1)} %fusion.135) | copy-start | bytes 28
  24.1 8.8 %copy-start.41 = (bf16[4]{0:T(256)(128)(2,1)}, bf16[4]{0:T(256)(128)(2,1)S(1)}, u32[]{:S(2)}) copy-start(bf16[4]{0:T(256)(128)(2,1)S(1)} %get-tuple-element.68) | copy-start | bytes 28
  29.6 5.2 %copy-start.48 = (bf16[8]{0:T(256)(128)(2,1)S(1)}, bf16[8]{0:T(256)(128)(2,1)}, u32[]{:S(2)}) copy-start(bf16[8]{0:T(256)(128)(2,1)} %fusion.134) | copy-start | bytes 52
  29.8 5.0 %copy-start.49 = (bf16[8]{0:T(256)(128)(2,1)S(1)}, bf16[8]{0:T(256)(128)(2,1)}, u32[]{:S(2)}) copy-start(bf16[8]{0:T(256)(128)(2,1)} %fusion.133) | copy-start | bytes 52
  32.9 11.4 %copy-start.12 = (bf16[8,8,4,384]{3,1,2,0:T(8,128)(2,1)}, bf16[8,8,4,384]{3,1,2,0:T(8,128)(2,1)S(1)}, u32[]{:S(2)}) copy-start(bf16[8,8,4,384]{3,1,2,0:T(8,128)(2,1)S(1)} %copy.73) | copy-start | bytes 589828
  33.0 11.1 %copy-start.14 = (bf16[8,8,4,384]{3,1,2,0:T(8,128)(2,1)}, bf16[8,8,4,384]{3,1,2,0:T(8,128)(2,1)S(1)}, u32[]{:S(2)}) copy-start(bf16[8,8,4,384]{3,1,2,0:T(8,128)(2,1)S(1)} %copy.72) | copy-start | bytes 589828
  33.7 9.6 %copy-start.32 = (bf16[4]{0:T(256)(128)(2,1)S(1)}, bf16[4]{0:T(256)(128)(2,1)}, u32[]{:S(2)}) copy-start(bf16[4]{0:T(256)(128)(2,1)} %get-tuple-element.61) | copy-start | bytes 28
  38.0 3.2 %collective-permute-start = (bf16[2,32,64]{2,1,0:T(8,128)(2,1)S(1)}, bf16[2,32,64]{2,1,0:T(8,128)(2,1)S(1)}, u32[]{:S(2)}, u32[]{:S(2)}) collective-permute-start(bf16[2,32,64]{2,1,0:T(8,128)(2,1)S(1)} %slice.234), channel_id=1, source_target_pairs={{0,8},{8,16},{16,24},{24,32},{32,40},{40,48},{48,56},{56,64},{64,7... | collective-permute-start | bytes 24584 | tf_op jit(solution)/shard_map/ppermute | solution.py:12
  47.8 6.1 %copy-start.23 = (f32[1536]{0:T(1024)S(1)}, f32[1536]{0:T(1024)}, u32[]{:S(2)}) copy-start(f32[1536]{0:T(1024)} %mul.710) | copy-start | bytes 18436
  49.4 12.9 %collective-permute-start.1 = (bf16[2,128,384]{2,1,0:T(8,128)(2,1)}, bf16[2,128,384]{2,1,0:T(8,128)(2,1)}, u32[]{:S(2)}, u32[]{:S(2)}) collective-permute-start(bf16[2,128,384]{2,1,0:T(8,128)(2,1)} %slice.237), channel_id=1, source_target_pairs={{0,8},{8,16},{16,24},{24,32},{32,40},{40,48},{48,56},{56,64},{64,7... | collective-permute-start | bytes 589832 | tf_op jit(solution)/shard_map/ppermute | solution.py:12
  55.6 6.8 %copy-start.33 = (bf16[4]{0:T(256)(128)(2,1)S(1)}, bf16[4]{0:T(256)(128)(2,1)}, u32[]{:S(2)}) copy-start(bf16[4]{0:T(256)(128)(2,1)} %get-tuple-element.61) | copy-start | bytes 28
  55.6 6.8 %copy-start.34 = (bf16[4]{0:T(256)(128)(2,1)S(1)}, bf16[4]{0:T(256)(128)(2,1)}, u32[]{:S(2)}) copy-start(bf16[4]{0:T(256)(128)(2,1)} %get-tuple-element.62) | copy-start | bytes 28
  64.7 4.9 %collective-permute-start.2 = (bf16[2,128,384]{2,1,0:T(8,128)(2,1)S(1)}, bf16[2,128,384]{2,1,0:T(8,128)(2,1)S(1)}, u32[]{:S(2)}, u32[]{:S(2)}) collective-permute-start(bf16[2,128,384]{2,1,0:T(8,128)(2,1)S(1)} %slice.240), channel_id=1, source_target_pairs={{0,8},{8,16},{16,24},{24,32},{32,40},{40,48},{48,56},{56,64},{64,7... | collective-permute-start | bytes 589832 | tf_op jit(solution)/shard_map/ppermute | solution.py:12
  69.7 6.1 %copy-start.40 = (f32[96]{0:T(128)S(1)}, f32[96]{0:T(128)}, u32[]{:S(2)}) copy-start(f32[96]{0:T(128)} %param.19) | copy-start | bytes 1156
  69.8 6.1 %copy-start.47 = (bf16[4,2]{1,0:T(4,128)(2,1)S(1)}, bf16[4,2]{1,0:T(4,128)(2,1)}, u32[]{:S(2)}) copy-start(bf16[4,2]{1,0:T(4,128)(2,1)} %convert_convert_fusion) | copy-start | bytes 52
  83.7 5.8 %copy-start.19 = (bf16[1024,96]{0,1:T(8,128)(2,1)S(1)}, bf16[1024,96]{0,1:T(8,128)(2,1)}, u32[]{:S(2)}) copy-start(bf16[1024,96]{0,1:T(8,128)(2,1)} %mul.743) | copy-start | bytes 589828
  83.7 7.6 %copy-start.42 = (bf16[8]{0:T(256)(128)(2,1)S(1)}, bf16[8]{0:T(256)(128)(2,1)}, u32[]{:S(2)}) copy-start(bf16[8]{0:T(256)(128)(2,1)} %get-tuple-element.59) | copy-start | bytes 52
  83.7 7.6 %copy-start.43 = (bf16[8]{0:T(256)(128)(2,1)S(1)}, bf16[8]{0:T(256)(128)(2,1)}, u32[]{:S(2)}) copy-start(bf16[8]{0:T(256)(128)(2,1)} %get-tuple-element.60) | copy-start | bytes 52
  85.7 10.6 %copy-start.35 = (bf16[4]{0:T(256)(128)(2,1)S(1)}, bf16[4]{0:T(256)(128)(2,1)}, u32[]{:S(2)}) copy-start(bf16[4]{0:T(256)(128)(2,1)} %fusion.137) | copy-start | bytes 28
  85.7 10.6 %copy-start.36 = (bf16[4]{0:T(256)(128)(2,1)S(1)}, bf16[4]{0:T(256)(128)(2,1)}, u32[]{:S(2)}) copy-start(bf16[4]{0:T(256)(128)(2,1)} %fusion.136) | copy-start | bytes 28
  85.7 10.6 %copy-start.39 = (bf16[4]{0:T(256)(128)(2,1)S(1)}, bf16[4]{0:T(256)(128)(2,1)}, u32[]{:S(2)}) copy-start(bf16[4]{0:T(256)(128)(2,1)} %copy-done.38) | copy-start | bytes 28
  85.7 5.6 %collective-permute-start.3 = (bf16[2,128,96]{1,2,0:T(8,128)(2,1)S(1)}, bf16[2,128,96]{1,2,0:T(8,128)(2,1)S(1)}, u32[]{:S(2)}, u32[]{:S(2)}) collective-permute-start(bf16[2,128,96]{1,2,0:T(8,128)(2,1)S(1)} %slice.243), channel_id=1, source_target_pairs={{0,8},{8,16},{16,24},{24,32},{32,40},{40,48},{48,56},{56,64},{64,7... | collective-permute-start | bytes 147464 | tf_op jit(solution)/shard_map/ppermute | solution.py:12
  89.8 6.2 %collective-permute-start.5 = (bf16[4,128,96]{1,2,0:T(8,128)(2,1)S(1)}, bf16[4,128,96]{1,2,0:T(8,128)(2,1)S(1)}, u32[]{:S(2)}, u32[]{:S(2)}) collective-permute-start(bf16[4,128,96]{1,2,0:T(8,128)(2,1)S(1)} %slice.248), channel_id=1, source_target_pairs={{8,0},{16,8},{24,16},{32,24},{40,32},{48,40},{56,48},{64,56},{72,6... | collective-permute-start | bytes 294920 | tf_op jit(solution)/shard_map/ppermute | solution.py:12
  91.4 5.2 %copy-start.17 = (bf16[3,384,192]{1,2,0:T(8,128)(2,1)S(1)}, bf16[3,384,192]{1,2,0:T(8,128)(2,1)}, u32[]{:S(2)}) copy-start(bf16[3,384,192]{1,2,0:T(8,128)(2,1)} %param.18) | copy-start | bytes 1327108
  97.0 5.0 %copy-start.45 = (bf16[512]{0:T(512)(128)(2,1)S(1)}, bf16[512]{0:T(512)(128)(2,1)}, u32[]{:S(2)}) copy-start(bf16[512]{0:T(512)(128)(2,1)} %broadcast_bitcast_fusion) | copy-start | bytes 3076
  100.6 8.2 %copy-start.8 = (bf16[3,384,384]{2,1,0:T(8,128)(2,1)S(1)}, bf16[3,384,384]{2,1,0:T(8,128)(2,1)}, u32[]{:S(2)}) copy-start(bf16[3,384,384]{2,1,0:T(8,128)(2,1)} %param.17) | copy-start | bytes 2654212
  100.6 8.6 %copy-start.6 = (f32[512,384]{1,0:T(8,128)S(1)}, f32[512,384]{1,0:T(8,128)}, u32[]{:S(2)}) copy-start(f32[512,384]{1,0:T(8,128)} %reshape.562) | copy-start | bytes 2359300
  100.6 8.7 %copy-start.44 = (f32[512]{0:T(512)S(1)}, f32[512]{0:T(512)}, u32[]{:S(2)}) copy-start(f32[512]{0:T(512)} %get-tuple-element.48) | copy-start | bytes 6148
  100.6 7.0 %collective-permute-start.6 = (bf16[2,128,384]{2,1,0:T(8,128)(2,1)S(1)}, bf16[2,128,384]{2,1,0:T(8,128)(2,1)S(1)}, u32[]{:S(2)}, u32[]{:S(2)}) collective-permute-start(bf16[2,128,384]{2,1,0:T(8,128)(2,1)S(1)} %bitcast.301), channel_id=1, source_target_pairs={{8,0},{16,8},{24,16},{32,24},{40,32},{48,40},{56,48},{64,56},{72,6... | collective-permute-start | bytes 589832 | tf_op jit(solution)/shard_map/ppermute | solution.py:12
  112.8 5.1 %copy-start.20 = (bf16[8,8,4,384]{3,1,2,0:T(8,128)(2,1)S(1)}, bf16[8,8,4,384]{3,1,2,0:T(8,128)(2,1)}, u32[]{:S(2)}) copy-start(bf16[8,8,4,384]{3,1,2,0:T(8,128)(2,1)} %copy.71) | copy-start | bytes 589828
  115.5 7.9 %collective-permute-start.7 = (bf16[2,128,384]{2,1,0:T(8,128)(2,1)}, bf16[2,128,384]{2,1,0:T(8,128)(2,1)}, u32[]{:S(2)}, u32[]{:S(2)}) collective-permute-start(bf16[2,128,384]{2,1,0:T(8,128)(2,1)} %slice.255), channel_id=1, source_target_pairs={{8,0},{16,8},{24,16},{32,24},{40,32},{48,40},{56,48},{64,56},{72,6... | collective-permute-start | bytes 589832 | tf_op jit(solution)/shard_map/ppermute | solution.py:12
  118.0 5.5 %copy-start.10 = (bf16[4,128,384]{2,1,0:T(8,128)(2,1)S(1)}, bf16[4,128,384]{2,1,0:T(8,128)(2,1)}, u32[]{:S(2)}) copy-start(bf16[4,128,384]{2,1,0:T(8,128)(2,1)} %copy-done.9) | copy-start | bytes 1179652
  120.9 11.5 %copy-start.27 = (f32[4,64]{1,0:T(4,128)S(1)}, f32[4,64]{1,0:T(4,128)}, u32[]{:S(2)}) copy-start(f32[4,64]{1,0:T(4,128)} %copy-done.26) | copy-start | bytes 3076
  120.9 11.5 %copy-start.29 = (f32[4,64]{1,0:T(4,128)S(1)}, f32[4,64]{1,0:T(4,128)}, u32[]{:S(2)}) copy-start(f32[4,64]{1,0:T(4,128)} %copy-done.28) | copy-start | bytes 3076
  120.9 11.5 %copy-start.31 = (f32[2560]{0:T(1024)S(1)}, f32[2560]{0:T(1024)}, u32[]{:S(2)}) copy-start(f32[2560]{0:T(1024)} %copy-done.30) | copy-start | bytes 30724
  134.7 6.3 %copy-start.4 = (f32[4,128,2,96]{1,3,2,0:T(8,128)S(1)}, f32[4,128,2,96]{1,3,2,0:T(8,128)}, u32[]{:S(2)}) copy-start(f32[4,128,2,96]{1,3,2,0:T(8,128)} %copy.122) | copy-start | bytes 1179652
  134.7 6.3 %copy-start.18 = (f32[12,8,8,128]{3,2,1,0:T(8,128)S(1)}, f32[12,8,8,128]{3,2,1,0:T(8,128)}, u32[]{:S(2)}) copy-start(f32[12,8,8,128]{3,2,1,0:T(8,128)} %copy.75) | copy-start | bytes 1179652
  (11 other events, 28.2 us)
Sparse Core Ops, SparseCore 0:
  21.2 16.0 reduce-scatter.1
where the time goes:
time: 271 us; the launch traced here: 270 us
  blocking collectives  135 us (50%)
  local copies, waits for them, and re-layouts  34.8 us (13%)
  other arithmetic  31.9 us (12%)
  matrix products  20.5 us (8%)
  starting transfers between devices  18 us (7%)
  between operations  15.8 us (6%)
  waiting for transfers between devices  13.7 us (5%)
    psum x1, blocking collectives, body(): total = lax.psum(jnp.sum(token_grad * token_grad), ('sec', 'frm', 'clip'))  117 us
    ppermute x8, starting transfers between devices, shifted_2(): return lax.ppermute(block, axis, route)  18 us
    ppermute x8, waiting for transfers between devices, shifted_2(): return lax.ppermute(block, axis, route)  11.9 us
    dot_general x12, matrix products, causal_back(): jnp.dot(shifted.reshape(length * pixels, -1), weight[offset].T, preferred...  10.5 us
    psum x1, blocking collectives, body(): lax.psum((jnp.sum(values, axis=-1, keepdims=True), jnp.sum(values * value...  9.01 us
    convert_element_type x4, local copies, waits for them, and re-layouts, decode_forward(): upsampled.astype(jnp.float32)  7.78 us
    all_gather x1, blocking collectives, body(): piece = lax.all_gather(latent_grad, 'sec', axis=1, tiled=True)  6.67 us
    dot_general x12, matrix products, causal(): jnp.dot(shifted.reshape(length * pixels, -1), weight[offset], preferred_e...  6.43 us
  transfers between devices with their start and end apart: 9, of which 5 were waited for; matrix products, arithmetic and copies ran while one was open for 11% of the time, Pallas kernels for 0%

commit v1 on v0

v1 whole, which is shorter than its diff:
```python
import functools

import jax
import jax.numpy as jnp
from jax import lax
from jax.experimental import pallas as pl
from jax.experimental.pallas import tpu as pltpu
from jax.sharding import PartitionSpec as P

BF = jnp.bfloat16
F32 = jnp.float32
MESH = pl.DeviceIdType.MESH
HI = 384
LO = 96
EPS = 1e-6
RB = 64


def nn(a, b):
    return jnp.dot(a, b, preferred_element_type=F32)


def nt(a, b):
    return lax.dot_general(a, b, (((1,), (1,)), ((), ())), preferred_element_type=F32)


def iota(shape, dim):
    return lax.broadcasted_iota(jnp.int32, shape, dim)


def one_hot(cond):
    return jnp.where(cond, 1.0, 0.0).astype(BF)


def sigmoid(x):
    return 0.5 * jnp.tanh(0.5 * x) + 0.5


def tile(mask, times):
    return jnp.concatenate([mask] * times, axis=1)


def nb(x, gain, width):
    r = lax.rsqrt(jnp.sum(x * x, axis=-1, keepdims=True) * (1.0 / width) + EPS)
    n = x * r * gain
    return n * sigmoid(n)


def nb_back(g, x, gain, width):
    r = lax.rsqrt(jnp.sum(x * x, axis=-1, keepdims=True) * (1.0 / width) + EPS)
    n = x * r * gain
    sg = sigmoid(n)
    u = g * sg * (1.0 + n * (1.0 - sg)) * gain
    mixed = jnp.sum(u * x, axis=-1, keepdims=True) * (1.0 / width)
    return r * u - x * (r * r * r * mixed)


def main_kernel(
    nf, nc, dd, count,
    hidden, mod, head_w, ids, w_in, gain1, w_one, w_up, gain2, w_two, reward,
    coef, wr, rd,
    HX, HW, W1, WUR, RWI, XS, XR, X2, RX, SRC, SR, RW, LTS, MT, MS, REP, WD, WI, WUP, G2,
    B, AC, TR, U, UP, A2, DEC, HS, UG, JL, TG, BG, ZM, PS, X3, RXA, ZS, ZB, ST,
    lsem, sec_s, sec_r, lat_s, lat_r, rew_s, rew_r, dec_s, dec_r, lg_s, lg_r, sx_s, sx_r, z_s, z_r,
):
    sec = lax.axis_index("sec")
    frm = lax.axis_index("frm")
    clip = lax.axis_index("clip")
    rows = 16 * nf
    line = 4 * nf
    hr = 8 * nf
    steps = rows // RB

    loads = [
        pltpu.make_async_copy(head_w, HW, lsem.at[0]),
        pltpu.make_async_copy(hidden, HX.at[pl.ds(0, hr)], lsem.at[1]),
        pltpu.make_async_copy(reward, RWI, lsem.at[2]),
        pltpu.make_async_copy(w_up, WUR, lsem.at[3]),
        pltpu.make_async_copy(w_one, W1, lsem.at[4]),
    ]
    for load in loads:
        load.start()

    barrier = pltpu.get_barrier_semaphore()

    def greet_frm(q, c):
        pl.semaphore_signal(barrier, inc=1, device_id=(sec, lax.rem(frm + q, nf), clip), device_id_type=MESH)
        return c

    lax.fori_loop(1, nf, greet_frm, 0)

    def cross(q):
        other = lax.rem(sec * nc + clip + q, 2 * nc)
        return (other // nc, frm, lax.rem(other, nc))

    def greet_cross(q, c):
        pl.semaphore_signal(barrier, inc=1, device_id=cross(q), device_id_type=MESH)
        return c

    lax.fori_loop(1, 2 * nc, greet_cross, 0)

    def to_all(src, dst, ssem, rsem):
        def send(q, c):
            d = lax.rem(frm + q, nf)
            pltpu.make_async_remote_copy(
                src_ref=src.at[d], dst_ref=dst.at[frm], send_sem=ssem, recv_sem=rsem,
                device_id=(sec, d, clip), device_id_type=MESH,
            ).start()
            return c

        lax.fori_loop(1, nf, send, 0)

    def all_of(src, dst, ssem, rsem):
        return pltpu.make_async_remote_copy(
            src_ref=src.at[pl.ds(0, nf - 1)], dst_ref=dst.at[pl.ds(0, nf - 1)],
            send_sem=ssem, recv_sem=rsem, device_id=(sec, frm, clip), device_id_type=MESH,
        )

    HX[pl.ds(hr + 64, 16), :] = jnp.ones((16, HX.shape[1]), BF)
    HX[pl.ds(hr + 80, 48), :] = jnp.zeros((48, HX.shape[1]), BF)
    loads[0].wait()
    shift = mod[0:1, :]
    scaled = nt(one_hot(iota((64, 64), 0) == iota((64, 64), 1)), HW[...]) * (1.0 + mod[1:2, :])
    scaled = scaled.astype(BF)
    HX[pl.ds(hr, 64), :] = scaled
    wr[...] = scaled
    coarse = shift.astype(BF).astype(F32)
    pick = iota((16, HX.shape[1]), 0)
    pair = jnp.where(pick == 0, coarse, jnp.where(pick == 1, shift - coarse, 0.0)).astype(BF)
    shifted = nn(pair, HW[...])
    loads[1].wait()
    product = nt(HX[pl.ds(0, hr + 80), :], HX[pl.ds(hr, 128), :])
    XS[pl.ds(0, hr + 80), :] = product
    XS[pl.ds(hr + 72, 8), pl.ds(0, 64)] = jnp.broadcast_to(shifted[0:1, :] + shifted[1:2, :], (8, 64))

    def squares(b, c):
        at = pl.multiple_of(b * 16, 16)
        x = HX[pl.ds(at, 16), :].astype(F32)
        total = jnp.sum(x * x, axis=-1, keepdims=True)
        XS[pl.ds(at, 16), :] += jnp.where(iota((16, 128), 1) == 80, total, 0.0)
        return c

    lax.fori_loop(0, hr // 16, squares, 0)

    pl.semaphore_wait(barrier, nf - 1 + 2 * nc - 1)
    swap = pltpu.make_async_remote_copy(
        src_ref=XS, dst_ref=XR, send_sem=sec_s, recv_sem=sec_r,
        device_id=(1 - sec, frm, clip), device_id_type=MESH,
    )
    swap.start()

    when = iota((line, 128), 0)
    own = jnp.broadcast_to(ids[...].astype(F32), (128, line)).T
    mt1 = jnp.where((own == pltpu.roll(own, 1, 0)) & (when >= 1), 1.0, 0.0)
    mt2 = jnp.where((own == pltpu.roll(own, 2, 0)) & (when >= 2), 1.0, 0.0)
    mt1u = pltpu.roll(mt1, line - 1, 0)
    mt2u = pltpu.roll(mt2, line - 2, 0)
    masks = jnp.concatenate([mt1, mt2, mt1u, mt2u], axis=1)
    MT[...] = masks
    REP[...] = one_hot(iota((rows, line), 0) // 4 == iota((rows, line), 1))
    MS[...] = nn(REP[...], masks.astype(BF))

    WD[...] = jnp.zeros(WD.shape, BF)
    WD[pl.ds(0, LO), pl.ds(0, LO)] = w_two[0]
    WD[pl.ds(0, LO), pl.ds(128, LO)] = w_two[1]
    WD[pl.ds(128, LO), pl.ds(128, LO)] = w_two[0]
    WD[pl.ds(256, LO), pl.ds(0, LO)] = w_two[2]
    WD[pl.ds(384, LO), pl.ds(0, LO)] = w_two[1]
    WD[pl.ds(384, LO), pl.ds(128, LO)] = w_two[2]
    WI[...] = jnp.zeros(WI.shape, BF)
    for k in range(3):
        for s in range(4):
            WI[pl.ds(128 * k + 16 * s, 16), :] = w_in[k]
    G2[...] = jnp.zeros(G2.shape, F32)
    G2[:, pl.ds(0, LO)] = jnp.broadcast_to(gain2[...], (8, LO))
    U[:, pl.ds(0, 8), :] = jnp.zeros((3, 8, 256), F32)
    HS[pl.ds(rows, 8), :] = jnp.zeros((8, 512), F32)
    JL[pl.ds(rows, 8), :] = jnp.zeros((8, 3 * HI), F32)

    loads[2].wait()
    SRC[...] = jnp.zeros(SRC.shape, BF)
    for j in range(4):
        for i in range(2):
            SRC[pl.ds(j * 4 * nf, 4 * nf), pl.ds(128 * i, LO)] = RWI[2 * j + i]
    to_row = iota((rows, rows), 0)
    from_row = iota((rows, rows), 1)
    perm = one_hot(from_row == ((to_row & 15) // 4) * (4 * nf) + (to_row // 16) * 4 + (to_row & 3))
    SR[...] = nn(perm, SRC[...]).astype(BF).reshape(nf, 16, 256)
    loads[3].wait()
    lane = iota((2 * LO, 256), 1)
    place = one_hot(((lane & 127) < LO) & (iota((2 * LO, 256), 0) == (lane // 128) * LO + (lane & 127)))
    WUP[...] = nn(WUR[...], place).astype(BF)

    swap.wait()
    ST[...] = XS[...] + XR[...]
    consts = ST[pl.ds(hr + 64, 16), :]
    col_sum = consts[0:1, :]
    sw = consts[8:9, :]
    stats = ST[pl.ds(0, hr), :]
    mean = stats[:, 64:65] * (1.0 / dd)
    inv = lax.rsqrt(stats[:, 80:81] * (1.0 / dd) - mean * mean + EPS)
    hl = iota((hr, 128), 1)
    pay = jnp.where(hl < 64, inv * (stats - mean * col_sum), jnp.where(hl == 64, inv, 0.0))
    XS[pl.ds(0, hr), :] = pay
    for j in range(4):
        X2[:, j, :] = XS[pl.ds(pl.multiple_of(j * 2 * nf + sec * nf, 8) if nf % 8 == 0 else j * 2 * nf + sec * nf, nf), :]
    to_all(X2, RX, lat_s, lat_r)
    to_all(SR, RW, rew_s, rew_r)
    RX[pl.ds(frm, 1)] = X2[pl.ds(frm, 1)]
    RW[pl.ds(frm, 1)] = SR[pl.ds(frm, 1)]
    all_of(X2, RX, lat_s, lat_r).wait_recv()

    for j in range(4):
        LTS[pl.ds(j, nf, stride=4), :] = RX[:, j, :]
    tl = iota((line, 128), 1)
    lat = jnp.where(tl < 64, LTS[...] + sw, 0.0)
    lat = lat.astype(BF).astype(F32)
    cat = jnp.concatenate(
        [lat, MT[:, 0:128] * pltpu.roll(lat, 1, 0), MT[:, 128:256] * pltpu.roll(lat, 2, 0)], axis=1
    ).astype(BF)
    mine = ((iota((rows, HI), 1) & 127) // 16) == (iota((rows, HI), 0) & 3)
    spread = jnp.where(mine, nn(REP[...], cat), 0.0).astype(BF)
    B[...] = nn(spread, WI[...])
    g1 = gain1[...]

    def act_one(b, carry):
        at = pl.multiple_of(b * RB, RB)
        act = nb(B[pl.ds(at, RB), :], g1, HI)
        ext = jnp.concatenate([carry, act], axis=0)
        m1 = tile(MS[pl.ds(at, RB), 0:128], 3)
        m2 = tile(MS[pl.ds(at, RB), 128:256], 3)
        AC[pl.ds(at, RB), 0:HI] = act.astype(BF)
        AC[pl.ds(at, RB), HI : 2 * HI] = (ext[4 : RB + 4] * m1).astype(BF)
        AC[pl.ds(at, RB), 2 * HI : 3 * HI] = (ext[0:RB] * m2).astype(BF)
        return ext[RB:]

    lax.fori_loop(0, steps, act_one, jnp.zeros((8, HI), F32))
    loads[4].wait()
    TR[...] = (B[...] + nn(AC[...], W1[...])).astype(BF)
    for k in range(3):
        U[k, pl.ds(8, rows), :] = nn(TR[...], WUP[pl.ds(HI * k, HI), :])
    g2 = G2[0:1, :]

    def act_two(b, carry):
        at = pl.multiple_of(b * RB, RB)
        m1 = tile(MS[pl.ds(at, RB), 0:128], 2)
        m2 = tile(MS[pl.ds(at, RB), 128:256], 2)
        one = U[1, pl.ds(at, RB + 8), :]
        two = U[2, pl.ds(at, RB + 8), :]
        up = U[0, pl.ds(at + 8, RB), :] + one[4 : RB + 4] * m1 + two[0:RB] * m2
        UP[pl.ds(at, RB), :] = up
        act = jnp.concatenate([nb(up[:, :128], g2, LO), nb(up[:, 128:], g2, LO)], axis=1)
        ext = jnp.concatenate([carry, act], axis=0)
        A2[pl.ds(at, RB), 0:256] = act.astype(BF)
        A2[pl.ds(at, RB), 256:512] = (ext[4 : RB + 4] * m1).astype(BF)
        return ext[RB:]

    lax.fori_loop(0, steps, act_two, jnp.zeros((8, 256), F32))
    DEC[...] = (UP[...] + nn(A2[...], WD[...])).astype(BF).reshape(nf, 16, 256)
    to_all(DEC, rd, dec_s, dec_r)
    keep = pltpu.make_async_copy(DEC.at[frm], rd.at[frm], lsem.at[5])
    keep.start()

    all_of(SR, RW, rew_s, rew_r).wait_recv()
    HS[pl.ds(0, rows), :] = nt(RW[...].reshape(rows, 256), WD[...])

    def up_grad(b, c):
        at = pl.multiple_of(b * RB, RB)
        m1 = tile(MS[pl.ds(at, RB), 256:384], 2)
        later = HS[pl.ds(at, RB + 8), 256:512]
        second = HS[pl.ds(at, RB), 0:256] + later[4 : RB + 4] * m1
        up = UP[pl.ds(at, RB), :]
        g = RW[pl.ds(b * (RB // 16), RB // 16)].reshape(RB, 256).astype(F32)
        back = [nb_back(second[:, i : i + 128], up[:, i : i + 128], g2, LO) for i in (0, 128)]
        UG[pl.ds(at, RB), :] = (g + jnp.concatenate(back, axis=1)).astype(BF)
        return c

    lax.fori_loop(0, steps, up_grad, 0)
    JL[pl.ds(0, rows), :] = nt(UG[...], WUP[...])

    def gathered(at):
        m1 = tile(MS[pl.ds(at, RB), 256:384], 3)
        m2 = tile(MS[pl.ds(at, RB), 384:512], 3)
        one = JL[pl.ds(at, RB + 8), HI : 2 * HI]
        two = JL[pl.ds(at, RB + 8), 2 * HI : 3 * HI]
        return JL[pl.ds(at, RB), 0:HI] + one[4 : RB + 4] * m1 + two[8 : RB + 8] * m2

    def trunk_grad(b, c):
        at = pl.multiple_of(b * RB, RB)
        TG[pl.ds(at, RB), :] = gathered(at).astype(BF)
        return c

    lax.fori_loop(0, steps, trunk_grad, 0)
    JL[pl.ds(0, rows), :] = nt(TG[...], W1[...])

    def base_grad(b, c):
        at = pl.multiple_of(b * RB, RB)
        back = nb_back(gathered(at), B[pl.ds(at, RB), :], g1, HI)
        BG[pl.ds(at, RB), :] = (TG[pl.ds(at, RB), :].astype(F32) + back).astype(BF)
        return c

    lax.fori_loop(0, steps, base_grad, 0)
    ZM[...] = jnp.where(mine, nt(BG[...], WI[...]), 0.0).astype(BF)
    rep_t = one_hot(iota((line, rows), 0) == iota((line, rows), 1) // 4)
    y = nn(rep_t, ZM[...])
    lg = y[:, 0:128]
    lg = lg + MT[:, 256:384] * pltpu.roll(y[:, 128:256], line - 1, 0)
    lg = lg + MT[:, 384:512] * pltpu.roll(y[:, 256:384], line - 2, 0)
    lgb = lg.astype(BF)
    lg = lgb.astype(F32)

    pre = LTS[...]
    inv_t = pre[:, 64:65]
    first = jnp.sum(lg * col_sum, axis=-1, keepdims=True) * (1.0 / dd)
    second = jnp.sum(lg * pre, axis=-1, keepdims=True) * (1.0 / dd)
    gram = ST[pl.ds(hr, 64), :]
    gram_hi = gram.astype(BF)
    gram_lo = (gram - gram_hi.astype(F32)).astype(BF)
    quad = nn(lgb[:, 0:64], gram_hi) + nn(lgb[:, 0:64], gram_lo)
    quad = jnp.sum(lg * quad, axis=-1, keepdims=True)
    inv_sq = inv_t * inv_t
    part = inv_sq * (quad - dd * (first * first + second * second * (1.0 + EPS * inv_sq)))
    part = jnp.sum(part, axis=0, keepdims=True)
    PS[...] = jnp.where(
        tl < 64, lg, jnp.where(tl == 64, first, jnp.where(tl == 65, second, jnp.where(tl == 66, part, 0.0)))
    )
    for j in range(4):
        X3[:, j, :] = PS[pl.ds(j, nf, stride=4), :]
    half = RXA.at[sec]
    to_all(X3, half, lg_s, lg_r)
    half[pl.ds(frm, 1)] = X3[pl.ds(frm, 1)]
    all_of(X3, half, lg_s, lg_r).wait_recv()

    trade = pltpu.make_async_remote_copy(
        src_ref=RXA.at[sec], dst_ref=RXA.at[sec], send_sem=sx_s, recv_sem=sx_r,
        device_id=(1 - sec, frm, clip), device_id_type=MESH,
    )
    trade.start()
    ZS[...] = jnp.broadcast_to(jnp.sum(half[:, 0, :], axis=0, keepdims=True), (8, 128))
    slot = sec * nc + clip

    def send_total(q, c):
        pltpu.make_async_remote_copy(
            src_ref=ZS, dst_ref=ZB.at[slot], send_sem=z_s, recv_sem=z_r,
            device_id=cross(q), device_id_type=MESH,
        ).start()
        return c

    lax.fori_loop(1, 2 * nc, send_total, 0)
    ZB[pl.ds(slot, 1)] = ZS[...].reshape(1, 8, 128)
    trade.wait()
    for j in range(4):
        for s in range(2):
            coef[pl.ds(j * 2 * nf + s * nf, nf), :] = RXA[s, :, j, :]
    z_all = pltpu.make_async_remote_copy(
        src_ref=ZB.at[pl.ds(0, 2 * nc - 1)], dst_ref=ZB.at[pl.ds(0, 2 * nc - 1)],
        send_sem=z_s, recv_sem=z_r, device_id=(sec, frm, clip), device_id_type=MESH,
    )
    z_all.wait_recv()
    total = jnp.sum(ZB[...], axis=0)[0:1, 66:67]
    grow = lax.rsqrt(jnp.maximum(total, 0.0) * (1.0 / count) + EPS)
    got = coef[...]
    a = got[:, 64:65]
    b = got[:, 65:66]
    stats = ST[pl.ds(0, hr), :]
    mean = stats[:, 64:65] * (1.0 / dd)
    inv = lax.rsqrt(stats[:, 80:81] * (1.0 / dd) - mean * mean + EPS)
    k0 = inv * grow
    k1 = k0 * (inv * b * mean - a)
    k2 = k0 * inv * b
    coef[...] = jnp.where(
        hl < 64, got, jnp.where(hl == 64, k0, jnp.where(hl == 65, k1, jnp.where(hl == 66, k2, 0.0)))
    )

    keep.wait()
    all_of(DEC, rd, dec_s, dec_r).wait_recv()
    all_of(X2, RX, lat_s, lat_r).wait_send()
    all_of(SR, RW, rew_s, rew_r).wait_send()
    all_of(DEC, rd, dec_s, dec_r).wait_send()
    all_of(X3, half, lg_s, lg_r).wait_send()
    z_all.wait_send()


def last_kernel(nf, coef, wr, hidden, rd, out, decoded):
    got = coef[...]
    grads = nn(got[:, 0:64].astype(BF), wr[...])
    out[...] = (grads * got[:, 64:65] + got[:, 65:66] - hidden[...].astype(F32) * got[:, 66:67]).astype(BF)

    @pl.when(pl.program_id(0) == 0)
    def _():
        rows = 16 * nf
        to_row = iota((rows, rows), 0)
        from_row = iota((rows, rows), 1)
        edge = 4 * nf
        perm = one_hot(from_row == ((lax.rem(to_row, edge)) // 4) * 16 + (to_row // edge) * 4 + (to_row & 3))
        back = nn(perm, rd[...].reshape(rows, 256)).astype(BF)
        for j in range(4):
            for i in range(2):
                decoded[2 * j + i] = back[j * edge : (j + 1) * edge, 128 * i : 128 * i + LO]


def body(nf, nc, dd, count, hidden, modulation, head_w, clip_ids, w_in, gain_one, w_one, w_up, gain_two, w_two, reward_grad):
    wide = hidden.shape[3]
    rows, line, hr = 16 * nf, 4 * nf, 8 * nf
    hid = hidden.reshape(hr, wide)
    anyspace = pl.BlockSpec(memory_space=pl.ANY)
    vm = pl.BlockSpec(memory_space=pltpu.VMEM)
    dma = pltpu.SemaphoreType.DMA
    V = pltpu.VMEM
    coef, wr, rd = pl.pallas_call(
        functools.partial(main_kernel, nf, nc, dd, count),
        out_shape=(
            jax.ShapeDtypeStruct((hr, 128), F32),
            jax.ShapeDtypeStruct((64, wide), BF),
            jax.ShapeDtypeStruct((nf, 16, 256), BF),
        ),
        in_specs=[anyspace, vm, anyspace, vm, vm, vm, anyspace, anyspace, vm, vm, anyspace],
        out_specs=(vm, vm, anyspace),
        scratch_shapes=[
            V((hr + 128, wide), BF),
            V((wide, 64), BF),
            V((3 * HI, HI), BF),
            V((3 * HI, 2 * LO), BF),
            V((8, 4 * nf, LO), BF),
            V((hr + 80, 128), F32),
            V((hr + 80, 128), F32),
            V((nf, 4, 128), F32),
            V((nf, 4, 128), F32),
            V((rows, 256), BF),
            V((nf, 16, 256), BF),
            V((nf, 16, 256), BF),
            V((line, 128), F32),
            V((line, 512), F32),
            V((rows, 512), F32),
            V((rows, line), BF),
            V((512, 256), BF),
            V((HI, HI), BF),
            V((3 * HI, 256), BF),
            V((8, 128), F32),
            V((rows, HI), F32),
            V((rows, 3 * HI), BF),
            V((rows, HI), BF),
            V((3, rows + 8, 256), F32),
            V((rows, 256), F32),
            V((rows, 512), BF),
            V((nf, 16, 256), BF),
            V((rows + 8, 512), F32),
            V((rows, 256), BF),
            V((rows + 8, 3 * HI), F32),
            V((rows, HI), BF),
            V((rows, HI), BF),
            V((rows, HI), BF),
            V((line, 128), F32),
            V((nf, 4, 128), F32),
            V((2, nf, 4, 128), F32),
            V((8, 128), F32),
            V((2 * nc, 8, 128), F32),
            V((hr + 80, 128), F32),
            dma((6,)),
        ]
        + [dma] * 14,
        compiler_params=pltpu.CompilerParams(
            collective_id=0, has_side_effects=True, vmem_limit_bytes=48 * 1024 * 1024
        ),
        name="exchange",
    )(
        hid, modulation[0], head_w, clip_ids, w_in, gain_one[None], w_one.reshape(3 * HI, HI),
        w_up.reshape(3 * HI, 2 * LO), gain_two[None], w_two, reward_grad[0],
    )
    cut = 512 if wide % 512 == 0 else wide
    grad, decoded = pl.pallas_call(
        functools.partial(last_kernel, nf),
        grid=(wide // cut,),
        out_shape=(
            jax.ShapeDtypeStruct((hr, wide), BF),
            jax.ShapeDtypeStruct((8, 4 * nf, LO), BF),
        ),
        in_specs=[
            pl.BlockSpec((hr, 128), lambda i: (0, 0)),
            pl.BlockSpec((64, cut), lambda i: (0, i)),
            pl.BlockSpec((hr, cut), lambda i: (0, i)),
            pl.BlockSpec((nf, 16, 256), lambda i: (0, 0, 0)),
        ],
        out_specs=(
            pl.BlockSpec((hr, cut), lambda i: (0, i)),
            pl.BlockSpec((8, 4 * nf, LO), lambda i: (0, 0, 0)),
        ),
        compiler_params=pltpu.CompilerParams(vmem_limit_bytes=32 * 1024 * 1024),
        name="finish",
    )(coef, wr, hid, rd)
    return decoded[None], grad.reshape(hidden.shape)


def solution(mesh):
    nf, nc = mesh.shape["frm"], mesh.shape["clip"]

    def whole(hidden, *rest):
        dd = hidden.shape[3]
        count = float(hidden.size)
        in_specs = (
            P("clip", "frm", None, "sec"),
            P("clip", None, "sec"),
            P("sec", None),
            P("clip", None),
            P(),
            P(),
            P(),
            P(),
            P(),
            P(),
            P("clip", "frm", "sec", None),
        )
        out_specs = (P("clip", "frm", "sec", None), P("clip", "frm", None, "sec"))
        return jax.shard_map(
            functools.partial(body, nf, nc, dd, count),
            mesh=mesh, in_specs=in_specs, out_specs=out_specs, check_vma=False,
        )(hidden, *rest)

    return whole
```

time: 271 us -> 58.2 us (0.21)
  blocking collectives: 135 us -> 0 us
  Pallas kernels: 0 us -> 51.7 us
  other arithmetic: 31.9 us -> 0 us
  local copies, waits for them, and re-layouts: 34.8 us -> 5.49 us
  matrix products: 20.5 us -> 0 us
  starting transfers between devices: 18 us -> 0 us
  between operations: 15.8 us -> 0.78 us
  waiting for transfers between devices: 13.7 us -> 0 us
    psum x3 -> x0, blocking collectives: 128 us -> none  [the longest x1 117 us: body(): total = lax.psum(jnp.sum(token_grad * token_grad), ('sec', 'frm', 'clip'))]
    pallas_call x0 -> x2, Pallas kernels: none -> 51.7 us  [the longest x1 48.4 us: body(): pl.pallas_call(functools.partial(main_kernel, nf, nc, dd, count), out_sha...]
    dot_general x26 -> x0, matrix products: 20.5 us -> none  [the longest x12 10.5 us: causal_back(): jnp.dot(shifted.reshape(length * pixels, -1), weight[offset].T, preferred...]
    ppermute x8 -> x0, starting transfers between devices: 18 us -> none  [shifted_2(): return lax.ppermute(block, axis, route)]
    mul x22 -> x0, local copies, waits for them, and re-layouts: 14.4 us -> none  [the longest x6 5.93 us: causal(): extended[2 - offset:2 - offset + length]]
    ppermute x8 -> x0, waiting for transfers between devices: 11.9 us -> none  [shifted_2(): return lax.ppermute(block, axis, route)]
    convert_element_type x8 -> x0, local copies, waits for them, and re-layouts: 11.3 us -> none  [the longest x4 7.78 us: decode_forward(): upsampled.astype(jnp.float32)]
    reduce_sum x9 -> x0, other arithmetic: 9.1 us -> none  [the longest x1 3.67 us: body(): total = lax.psum(jnp.sum(token_grad * token_grad), ('sec', 'frm', 'clip'))]
  transfers between devices with their start and end apart: 9 -> 0, of which waited for: 5 -> 0; matrix products, arithmetic and copies ran while one was open for 11% -> 0% of each run, Pallas kernels for 0% -> 0%
where the time goes in v1:
time: 58.2 us; the launch traced here: 57.9 us
  Pallas kernels  51.7 us (89%)
  local copies, waits for them, and re-layouts  5.49 us (9%)
  between operations  0.78 us (1%)
    pallas_call x1, Pallas kernels, body(): pl.pallas_call(functools.partial(main_kernel, nf, nc, dd, count), out_sha...  48.4 us
    unnamed x20, local copies, waits for them, and re-layouts  4.68 us
    pallas_call x1, Pallas kernels, body(): pl.pallas_call(functools.partial(last_kernel, nf), grid=(wide // cut,), o...  3.26 us

profile of v1, /device:TPU:1, one launch (start us, length us, event | category | flops | bytes accessed | tf_op | source)
XLA Modules:
  0.0 57.9 jit_solution(18244239295939614453)
XLA Ops:
  0.6 0.0 copy-start.2
  0.6 0.0 copy-start.6
  0.7 0.0 copy-start.3
  0.7 0.0 copy-start.5
  0.7 0.0 copy-start.7
  0.7 0.0 copy-start.4
  0.7 0.0 copy-start
  0.7 0.8 %broadcast_in_dim.9.gain1 = f32[1,384]{1,0:T(1,128)S(1)} reshape(f32[384]{0:T(512)} %param.16) | data formatting | bytes 3072 | tf_op jit(solution)/shard_map/broadcast_in_dim | solution.py:467
  1.5 1.1 %copy.14 = bf16[1,8,128,96]{3,2,1,0:T(8,128)(2,1)S(1)} copy(bf16[1,8,128,96]{2,3,1,0:T(8,128)(2,1)} %param.21) | data formatting | bytes 393216 | tf_op args[10]
  2.6 1.3 %copy.13 = bf16[3,384,192]{2,1,0:T(8,128)(2,1)S(1)} copy(bf16[3,384,192]{1,2,0:T(8,128)(2,1)} %param.18) | data formatting | bytes 884736 | tf_op args[7]
  3.9 0.0 copy-done.7
  3.9 0.3 copy.15.head_w
  4.2 0.0 copy-done.2
  4.2 0.0 copy-done.6
  4.2 0.0 copy-done.3
  4.2 0.0 copy-done.5
  4.2 0.0 copy-done.4
  4.3 0.0 copy-done
  4.3 0.0 copy-start.1
  4.3 1.2 %copy-done.1 = bf16[3,384,384]{2,1,0:T(8,128)(2,1)S(1)} copy-done((bf16[3,384,384]{2,1,0:T(8,128)(2,1)S(1)}, bf16[3,384,384]{2,1,0:T(8,128)(2,1)}, u32[]{:S(2)}) %copy-start.1) | copy-done | bytes 884760
  5.4 48.4 %exchange.1 = (f32[256,128]{1,0:T(8,128)S(1)}, bf16[64,2560]{1,0:T(8,128)(2,1)S(1)}, bf16[32,16,256]{2,1,0:T(8,128)(2,1)S(1)}) custom-call(bf16[256,2560]{1,0:T(8,128)(2,1)S(1)} %bitcast.8, f32[2,2560]{1,0:T(2,128)S(1)} %bitcast.14, bf16[2560,64]{1,0:T(8,128)(2,1)S(1)} %copy.15.head_w, s32[1,128]{1,0:T(1,128)S(1)} %copy-done.5, ...), custom_call_target="tpu_custom_call" | custom-call | tf_op jit(solution)/shard_map/exchange/pallas_call | solution.py:410
  53.9 3.3 %finish.1 = (bf16[256,2560]{1,0:T(8,128)(2,1)}, bf16[8,128,96]{2,1,0:T(8,128)(2,1)S(1)}) custom-call(f32[256,128]{1,0:T(8,128)S(1)} %get-tuple-element.7.coef, bf16[64,2560]{1,0:T(8,128)(2,1)S(1)} %get-tuple-element.8.wr, bf16[256,2560]{1,0:T(8,128)(2,1)S(1)} %bitcast.9, bf16[32,16,256]{2,1,0:T(8,128)(2,1)S(1)} %get-tuple-element.9.rd), custom_call_target="tpu_custom_call" | custom-call | tf_op jit(solution)/shard_map/finish/pallas_call | solution.py:471
  57.1 0.8 %copy.16 = bf16[1,8,128,96]{2,3,1,0:T(8,128)(2,1)} copy(bf16[1,8,128,96]{3,2,1,0:T(8,128)(2,1)S(1)} %bitcast.13) | data formatting | bytes 393216
Async XLA Ops:
  0.6 3.6 %copy-start.2 = (bf16[3,96,96]{2,1,0:T(8,128)(2,1)S(1)}, bf16[3,96,96]{2,1,0:T(8,128)(2,1)}, u32[]{:S(2)}) copy-start(bf16[3,96,96]{2,1,0:T(8,128)(2,1)} %w_two.1) | copy-start | bytes 165892
  0.6 3.6 %copy-start.6 = (f32[96]{0:T(128)S(1)}, f32[96]{0:T(128)}, u32[]{:S(2)}) copy-start(f32[96]{0:T(128)} %param.19) | copy-start | bytes 1156
  0.7 3.6 %copy-start.3 = (bf16[3,16,384]{2,1,0:T(8,128)(2,1)S(1)}, bf16[3,16,384]{2,1,0:T(8,128)(2,1)}, u32[]{:S(2)}) copy-start(bf16[3,16,384]{2,1,0:T(8,128)(2,1)} %w_in.1) | copy-start | bytes 110596
  0.7 3.6 %copy-start.5 = (s32[1,128]{1,0:T(1,128)S(1)}, s32[1,128]{1,0:T(1,128)}, u32[]{:S(2)}) copy-start(s32[1,128]{1,0:T(1,128)} %ids.1) | copy-start | bytes 1540
  0.7 3.2 %copy-start.7 = (bf16[2560,64]{0,1:T(8,128)(2,1)S(1)}, bf16[2560,64]{0,1:T(8,128)(2,1)}, u32[]{:S(2)}) copy-start(bf16[2560,64]{0,1:T(8,128)(2,1)} %param.13) | copy-start | bytes 983044
  0.7 3.6 %copy-start.4 = (f32[1,2,2560]{2,1,0:T(2,128)S(1)}, f32[1,2,2560]{2,1,0:T(2,128)}, u32[]{:S(2)}) copy-start(f32[1,2,2560]{2,1,0:T(2,128)} %param.12) | copy-start | bytes 61444
  0.7 3.6 %copy-start = (bf16[1,4,64,2560]{3,2,1,0:T(8,128)(2,1)S(1)}, bf16[1,4,64,2560]{3,2,1,0:T(8,128)(2,1)}, u32[]{:S(2)}) copy-start(bf16[1,4,64,2560]{3,2,1,0:T(8,128)(2,1)} %param.11) | copy-start | bytes 3932164
  4.3 1.2 %copy-start.1 = (bf16[3,384,384]{2,1,0:T(8,128)(2,1)S(1)}, bf16[3,384,384]{2,1,0:T(8,128)(2,1)}, u32[]{:S(2)}) copy-start(bf16[3,384,384]{2,1,0:T(8,128)(2,1)} %param.17) | copy-start | bytes 2654212

commit v2 on v1

--- a/solution.py
+++ b/solution.py
@@ -58,9 +58,9 @@
 def main_kernel(
     nf, nc, dd, count,
     hidden, mod, head_w, ids, w_in, gain1, w_one, w_up, gain2, w_two, reward,
-    coef, wr, rd,
-    HX, HW, W1, WUR, RWI, XS, XR, X2, RX, SRC, SR, RW, LTS, MT, MS, REP, WD, WI, WUP, G2,
-    B, AC, TR, U, UP, A2, DEC, HS, UG, JL, TG, BG, ZM, PS, X3, RXA, ZS, ZB, ST,
+    raw, scale_out, dect,
+    HX, HW, W1, XS, XR, X2, RX, SRC, SR, RW, LTS, MT, MS, REP, WD, WI, WUP, G2,
+    B, AC, TR, U, UP, A2, DEC, HS, UG, JL, TG, BG, ZM, PS, X3, RXA, ZS, ZB, ST, RD, FIN, KB, RAW, DT,
     lsem, sec_s, sec_r, lat_s, lat_r, rew_s, rew_r, dec_s, dec_r, lg_s, lg_r, sx_s, sx_r, z_s, z_r,
 ):
     sec = lax.axis_index("sec")
@@ -71,44 +71,56 @@
     hr = 8 * nf
     steps = rows // RB
 
+    edge = 4 * nf
     loads = [
-        pltpu.make_async_copy(head_w, HW, lsem.at[0]),
-        pltpu.make_async_copy(hidden, HX.at[pl.ds(0, hr)], lsem.at[1]),
-        pltpu.make_async_copy(reward, RWI, lsem.at[2]),
-        pltpu.make_async_copy(w_up, WUR, lsem.at[3]),
-        pltpu.make_async_copy(w_one, W1, lsem.at[4]),
+        [pltpu.make_async_copy(head_w, HW, lsem.at[0])],
+        [pltpu.make_async_copy(hidden, HX.at[pl.ds(0, hr)], lsem.at[1])],
+        [
+            pltpu.make_async_copy(
+                reward.at[2 * j + i], SRC.at[pl.ds(128 * i, LO), pl.ds(j * edge, edge)], lsem.at[6 + 2 * j + i]
+            )
+            for j in range(4) for i in range(2)
+        ],
+        [
+            pltpu.make_async_copy(
+                w_up.at[k, pl.ds(LO * i, LO)], WUP.at[pl.ds(256 * k + 128 * i, LO)], lsem.at[14 + 2 * k + i]
+            )
+            for k in range(3) for i in range(2)
+        ],
+        [pltpu.make_async_copy(w_one, W1, lsem.at[4])],
     ]
-    for load in loads:
-        load.start()
+
+    def load(which):
+        for copy in loads[which]:
+            copy.wait()
+
+    for group in loads:
+        for copy in group:
+            copy.start()
+
+    nx = 4
+    ny = nf // nx
+    yy, xx = frm // nx, lax.rem(frm, nx)
+    far = sorted(
+        ((min(dy, ny - dy) + min(dx, nx - dx), dy, dx) for dy in range(ny) for dx in range(nx) if dy or dx),
+        reverse=True,
+    )
+    peers = [lax.rem(yy + dy, ny) * nx + lax.rem(xx + dx, nx) for _, dy, dx in far]
+    above = [lax.rem(clip + dz, nc) for dz in sorted(range(1, nc), key=lambda dz: -min(dz, nc - dz))]
 
     barrier = pltpu.get_barrier_semaphore()
-
-    def greet_frm(q, c):
-        pl.semaphore_signal(barrier, inc=1, device_id=(sec, lax.rem(frm + q, nf), clip), device_id_type=MESH)
-        return c
-
-    lax.fori_loop(1, nf, greet_frm, 0)
-
-    def cross(q):
-        other = lax.rem(sec * nc + clip + q, 2 * nc)
-        return (other // nc, frm, lax.rem(other, nc))
-
-    def greet_cross(q, c):
-        pl.semaphore_signal(barrier, inc=1, device_id=cross(q), device_id_type=MESH)
-        return c
-
-    lax.fori_loop(1, 2 * nc, greet_cross, 0)
+    for d in peers:
+        pl.semaphore_signal(barrier, inc=1, device_id=(sec, d, clip), device_id_type=MESH)
+    for d in above:
+        pl.semaphore_signal(barrier, inc=1, device_id=(sec, frm, d), device_id_type=MESH)
+    pl.semaphore_signal(barrier, inc=1, device_id=(1 - sec, frm, clip), device_id_type=MESH)
 
     def to_all(src, dst, ssem, rsem):
-        def send(q, c):
-            d = lax.rem(frm + q, nf)
+        for d in peers:
             pltpu.make_async_remote_copy(
                 src_ref=src.at[d], dst_ref=dst.at[frm], send_sem=ssem, recv_sem=rsem,
                 device_id=(sec, d, clip), device_id_type=MESH,
             ).start()
-            return c
-
-        lax.fori_loop(1, nf, send, 0)
 
     def all_of(src, dst, ssem, rsem):
         return pltpu.make_async_remote_copy(
@@ -118,31 +130,27 @@
 
     HX[pl.ds(hr + 64, 16), :] = jnp.ones((16, HX.shape[1]), BF)
     HX[pl.ds(hr + 80, 48), :] = jnp.zeros((48, HX.shape[1]), BF)
-    loads[0].wait()
+    load(0)
     shift = mod[0:1, :]
-    scaled = nt(one_hot(iota((64, 64), 0) == iota((64, 64), 1)), HW[...]) * (1.0 + mod[1:2, :])
-    scaled = scaled.astype(BF)
-    HX[pl.ds(hr, 64), :] = scaled
-    wr[...] = scaled
+    HX[pl.ds(hr, 64), :] = (HW[...].astype(F32) * (1.0 + mod[1:2, :])).astype(BF)
     coarse = shift.astype(BF).astype(F32)
     pick = iota((16, HX.shape[1]), 0)
     pair = jnp.where(pick == 0, coarse, jnp.where(pick == 1, shift - coarse, 0.0)).astype(BF)
-    shifted = nn(pair, HW[...])
-    loads[1].wait()
-    product = nt(HX[pl.ds(0, hr + 80), :], HX[pl.ds(hr, 128), :])
-    XS[pl.ds(0, hr + 80), :] = product
+    shifted = nt(pair, HW[...])
+    XS[pl.ds(hr, 80), :] = nt(HX[pl.ds(hr, 80), :], HX[pl.ds(hr, 128), :])
     XS[pl.ds(hr + 72, 8), pl.ds(0, 64)] = jnp.broadcast_to(shifted[0:1, :] + shifted[1:2, :], (8, 64))
 
-    def squares(b, c):
-        at = pl.multiple_of(b * 16, 16)
-        x = HX[pl.ds(at, 16), :].astype(F32)
+    load(1)
+    block = min(hr, 64)
+    for b in range(hr // block):
+        h = HX[pl.ds(b * block, block), :]
+        x = h.astype(F32)
         total = jnp.sum(x * x, axis=-1, keepdims=True)
-        XS[pl.ds(at, 16), :] += jnp.where(iota((16, 128), 1) == 80, total, 0.0)
-        return c
-
-    lax.fori_loop(0, hr // 16, squares, 0)
-
-    pl.semaphore_wait(barrier, nf - 1 + 2 * nc - 1)
+        XS[pl.ds(b * block, block), :] = nt(h, HX[pl.ds(hr, 128), :]) + jnp.where(
+            iota((block, 128), 1) == 80, total, 0.0
+        )
+
+    pl.semaphore_wait(barrier, nf - 1 + nc)
     swap = pltpu.make_async_remote_copy(
         src_ref=XS, dst_ref=XR, send_sem=sec_s, recv_sem=sec_r,
         device_id=(1 - sec, frm, clip), device_id_type=MESH,
@@ -172,24 +180,21 @@
         for s in range(4):
             WI[pl.ds(128 * k + 16 * s, 16), :] = w_in[k]
     G2[...] = jnp.zeros(G2.shape, F32)
-    G2[:, pl.ds(0, LO)] = jnp.broadcast_to(gain2[...], (8, LO))
-    U[:, pl.ds(0, 8), :] = jnp.zeros((3, 8, 256), F32)
+    G2[:, pl.ds(0, LO)] = jnp.broadcast_to(gain2[...].reshape(1, LO), (8, LO))
+    U[pl.ds(0, 8), :] = jnp.zeros((8, 768), F32)
     HS[pl.ds(rows, 8), :] = jnp.zeros((8, 512), F32)
     JL[pl.ds(rows, 8), :] = jnp.zeros((8, 3 * HI), F32)
 
-    loads[2].wait()
-    SRC[...] = jnp.zeros(SRC.shape, BF)
-    for j in range(4):
-        for i in range(2):
-            SRC[pl.ds(j * 4 * nf, 4 * nf), pl.ds(128 * i, LO)] = RWI[2 * j + i]
+    for i in range(2):
+        SRC[pl.ds(128 * i + LO, 128 - LO), :] = jnp.zeros((128 - LO, rows), BF)
+    for k in range(6):
+        WUP[pl.ds(128 * k + LO, 128 - LO), :] = jnp.zeros((128 - LO, HI), BF)
+    load(2)
     to_row = iota((rows, rows), 0)
     from_row = iota((rows, rows), 1)
-    perm = one_hot(from_row == ((to_row & 15) // 4) * (4 * nf) + (to_row // 16) * 4 + (to_row & 3))
-    SR[...] = nn(perm, SRC[...]).astype(BF).reshape(nf, 16, 256)
-    loads[3].wait()
-    lane = iota((2 * LO, 256), 1)
-    place = one_hot(((lane & 127) < LO) & (iota((2 * LO, 256), 0) == (lane // 128) * LO + (lane & 127)))
-    WUP[...] = nn(WUR[...], place).astype(BF)
+    perm = one_hot(from_row == ((to_row & 15) // 4) * edge + (to_row // 16) * 4 + (to_row & 3))
+    SR[...] = nt(perm, SRC[...]).astype(BF).reshape(nf, 16, 256)
+    load(3)
 
     swap.wait()
     ST[...] = XS[...] + XR[...]
@@ -221,7 +226,7 @@
     mine = ((iota((rows, HI), 1) & 127) // 16) == (iota((rows, HI), 0) & 3)
     spread = jnp.where(mine, nn(REP[...], cat), 0.0).astype(BF)
     B[...] = nn(spread, WI[...])
-    g1 = gain1[...]
+    g1 = gain1[...].reshape(1, HI)
 
     def act_one(b, carry):
         at = pl.multiple_of(b * RB, RB)
@@ -235,19 +240,18 @@
         return ext[RB:]
 
     lax.fori_loop(0, steps, act_one, jnp.zeros((8, HI), F32))
-    loads[4].wait()
+    load(4)
     TR[...] = (B[...] + nn(AC[...], W1[...])).astype(BF)
-    for k in range(3):
-        U[k, pl.ds(8, rows), :] = nn(TR[...], WUP[pl.ds(HI * k, HI), :])
+    U[pl.ds(8, rows), :] = nt(TR[...], WUP[...])
     g2 = G2[0:1, :]
 
     def act_two(b, carry):
         at = pl.multiple_of(b * RB, RB)
         m1 = tile(MS[pl.ds(at, RB), 0:128], 2)
         m2 = tile(MS[pl.ds(at, RB), 128:256], 2)
-        one = U[1, pl.ds(at, RB + 8), :]
-        two = U[2, pl.ds(at, RB + 8), :]
-        up = U[0, pl.ds(at + 8, RB), :] + one[4 : RB + 4] * m1 + two[0:RB] * m2
+        one = U[pl.ds(at, RB + 8), 256:512]
+        two = U[pl.ds(at, RB + 8), 512:768]
+        up = U[pl.ds(at + 8, RB), 0:256] + one[4 : RB + 4] * m1 + two[0:RB] * m2
         UP[pl.ds(at, RB), :] = up
         act = jnp.concatenate([nb(up[:, :128], g2, LO), nb(up[:, 128:], g2, LO)], axis=1)
         ext = jnp.concatenate([carry, act], axis=0)
@@ -257,9 +261,8 @@
 
     lax.fori_loop(0, steps, act_two, jnp.zeros((8, 256), F32))
     DEC[...] = (UP[...] + nn(A2[...], WD[...])).astype(BF).reshape(nf, 16, 256)
-    to_all(DEC, rd, dec_s, dec_r)
-    keep = pltpu.make_async_copy(DEC.at[frm], rd.at[frm], lsem.at[5])
-    keep.start()
+    to_all(DEC, RD, dec_s, dec_r)
+    RD[pl.ds(frm, 1)] = DEC[pl.ds(frm, 1)]
 
     all_of(SR, RW, rew_s, rew_r).wait_recv()
     HS[pl.ds(0, rows), :] = nt(RW[...].reshape(rows, 256), WD[...])
@@ -276,7 +279,8 @@
         return c
 
     lax.fori_loop(0, steps, up_grad, 0)
-    JL[pl.ds(0, rows), :] = nt(UG[...], WUP[...])
+    for k in range(3):
+        JL[pl.ds(0, rows), HI * k : HI * k + HI] = nn(UG[...], WUP[pl.ds(256 * k, 256), :])
 
     def gathered(at):
         m1 = tile(MS[pl.ds(at, RB), 256:384], 3)
@@ -336,97 +340,119 @@
         device_id=(1 - sec, frm, clip), device_id_type=MESH,
     )
     trade.start()
-    ZS[...] = jnp.broadcast_to(jnp.sum(half[:, 0, :], axis=0, keepdims=True), (8, 128))
-    slot = sec * nc + clip
-
-    def send_total(q, c):
+    trade.wait()
+    everyone = jnp.sum(RXA[0, :, 0, :] + RXA[1, :, 0, :], axis=0, keepdims=True)
+    ZS[...] = everyone
+    for d in above:
         pltpu.make_async_remote_copy(
-            src_ref=ZS, dst_ref=ZB.at[slot], send_sem=z_s, recv_sem=z_r,
-            device_id=cross(q), device_id_type=MESH,
+            src_ref=ZS, dst_ref=ZB.at[clip], send_sem=z_s, recv_sem=z_r,
+            device_id=(sec, frm, d), device_id_type=MESH,
         ).start()
-        return c
-
-    lax.fori_loop(1, 2 * nc, send_total, 0)
-    ZB[pl.ds(slot, 1)] = ZS[...].reshape(1, 8, 128)
-    trade.wait()
+    ZB[pl.ds(clip, 1)] = everyone.reshape(1, 1, 128)
+
     for j in range(4):
         for s in range(2):
-            coef[pl.ds(j * 2 * nf + s * nf, nf), :] = RXA[s, :, j, :]
-    z_all = pltpu.make_async_remote_copy(
-        src_ref=ZB.at[pl.ds(0, 2 * nc - 1)], dst_ref=ZB.at[pl.ds(0, 2 * nc - 1)],
-        send_sem=z_s, recv_sem=z_r, device_id=(sec, frm, clip), device_id_type=MESH,
-    )
-    z_all.wait_recv()
-    total = jnp.sum(ZB[...], axis=0)[0:1, 66:67]
-    grow = lax.rsqrt(jnp.maximum(total, 0.0) * (1.0 / count) + EPS)
-    got = coef[...]
+            FIN[pl.ds(j * 2 * nf + s * nf, nf), :] = RXA[s, :, j, :]
+    got = FIN[...]
     a = got[:, 64:65]
     b = got[:, 65:66]
     stats = ST[pl.ds(0, hr), :]
     mean = stats[:, 64:65] * (1.0 / dd)
     inv = lax.rsqrt(stats[:, 80:81] * (1.0 / dd) - mean * mean + EPS)
-    k0 = inv * grow
-    k1 = k0 * (inv * b * mean - a)
-    k2 = k0 * inv * b
-    coef[...] = jnp.where(
-        hl < 64, got, jnp.where(hl == 64, k0, jnp.where(hl == 65, k1, jnp.where(hl == 66, k2, 0.0)))
+    KB[0] = jnp.broadcast_to(inv, (hr, 128))
+    KB[1] = jnp.broadcast_to(inv * (inv * b * mean - a), (hr, 128))
+    KB[2] = jnp.broadcast_to(inv * inv * b, (hr, 128))
+    gotb = got[:, 0:64].astype(BF)
+
+    def token_grad(c, carry):
+        at = pl.ds(pl.multiple_of(c * 256, 256), 256)
+        grads = nn(gotb, HX[pl.ds(hr, 64), at])
+        h = HX[pl.ds(0, hr), at].astype(F32)
+        RAW[:, at] = (grads * tile(KB[0], 2) + tile(KB[1], 2) - h * tile(KB[2], 2)).astype(BF)
+        return carry
+
+    lax.fori_loop(0, HX.shape[1] // 256, token_grad, 0)
+    out_raw = pltpu.make_async_copy(RAW, raw, lsem.at[0])
+    out_raw.start()
+
+    all_of(DEC, RD, dec_s, dec_r).wait_recv()
+    same = one_hot(iota((256, 256), 0) == iota((256, 256), 1))
+    turned = nt(same, RD[...].reshape(rows, 256)).astype(BF)
+    perm = one_hot(to_row == ((from_row // edge) * 4) + (lax.rem(from_row, edge) // 4) * 16 + (from_row & 3))
+    turned = nn(turned, perm).astype(BF)
+    for j in range(4):
+        for i in range(2):
+            DT[2 * j + i] = turned[128 * i : 128 * i + LO, j * edge : (j + 1) * edge]
+
+    out_dec = pltpu.make_async_copy(DT, dect, lsem.at[1])
+    out_dec.start()
+
+    z_all = pltpu.make_async_remote_copy(
+        src_ref=ZB.at[pl.ds(0, nc - 1)], dst_ref=ZB.at[pl.ds(0, nc - 1)],
+        send_sem=z_s, recv_sem=z_r, device_id=(sec, frm, clip), device_id_type=MESH,
     )
-
-    keep.wait()
-    all_of(DEC, rd, dec_s, dec_r).wait_recv()
+    z_all.wait_recv()
+    total = jnp.sum(ZB[:, 0, :], axis=0, keepdims=True)[:, 66:67]
+    grow = lax.rsqrt(jnp.maximum(total, 0.0) * (1.0 / count) + EPS)
+    scale_out[...] = jnp.broadcast_to(grow, (8, 128))
+    out_raw.wait()
+    out_dec.wait()
+
     all_of(X2, RX, lat_s, lat_r).wait_send()
     all_of(SR, RW, rew_s, rew_r).wait_send()
-    all_of(DEC, rd, dec_s, dec_r).wait_send()
+    all_of(DEC, RD, dec_s, dec_r).wait_send()
     all_of(X3, half, lg_s, lg_r).wait_send()
     z_all.wait_send()
 
 
-def last_kernel(nf, coef, wr, hidden, rd, out, decoded):
-    got = coef[...]
-    grads = nn(got[:, 0:64].astype(BF), wr[...])
-    out[...] = (grads * got[:, 64:65] + got[:, 65:66] - hidden[...].astype(F32) * got[:, 66:67]).astype(BF)
-
-    @pl.when(pl.program_id(0) == 0)
-    def _():
-        rows = 16 * nf
-        to_row = iota((rows, rows), 0)
-        from_row = iota((rows, rows), 1)
-        edge = 4 * nf
-        perm = one_hot(from_row == ((lax.rem(to_row, edge)) // 4) * 16 + (to_row // edge) * 4 + (to_row & 3))
-        back = nn(perm, rd[...].reshape(rows, 256)).astype(BF)
-        for j in range(4):
-            for i in range(2):
-                decoded[2 * j + i] = back[j * edge : (j + 1) * edge, 128 * i : 128 * i + LO]
+def last_kernel(parts, raw, scale, dect, out, decoded, got, done, dec, sems):
+    size = got.shape[0] // parts
+    inward = pltpu.make_async_copy(dect, dec, sems.at[0])
+    outward = pltpu.make_async_copy(dec, decoded, sems.at[0])
+    spots = [pl.ds(p * size, size) for p in range(parts)]
+    reads = [pltpu.make_async_copy(raw.at[at], got.at[at], sems.at[1 + p]) for p, at in enumerate(spots)]
+    for read in reads:
+        read.start()
+    inward.start()
+    writes = []
+    for p, at in enumerate(spots):
+        reads[p].wait()
+        done[at, :] = (got[at, :].astype(F32) * scale[0:1, 0:1]).astype(BF)
+        writes.append(pltpu.make_async_copy(done.at[at], out.at[at], sems.at[1 + parts + p]))
+        writes[-1].start()
+    inward.wait()
+    outward.start()
+    for write in writes:
+        write.wait()
+    outward.wait()
 
 
 def body(nf, nc, dd, count, hidden, modulation, head_w, clip_ids, w_in, gain_one, w_one, w_up, gain_two, w_two, reward_grad):
     wide = hidden.shape[3]
     rows, line, hr = 16 * nf, 4 * nf, 8 * nf
     hid = hidden.reshape(hr, wide)
-    anyspace = pl.BlockSpec(memory_space=pl.ANY)
+    hbm = pl.BlockSpec(memory_space=pltpu.HBM)
     vm = pl.BlockSpec(memory_space=pltpu.VMEM)
     dma = pltpu.SemaphoreType.DMA
     V = pltpu.VMEM
-    coef, wr, rd = pl.pallas_call(
+    raw, scale, dect = pl.pallas_call(
         functools.partial(main_kernel, nf, nc, dd, count),
         out_shape=(
-            jax.ShapeDtypeStruct((hr, 128), F32),
-            jax.ShapeDtypeStruct((64, wide), BF),
-            jax.ShapeDtypeStruct((nf, 16, 256), BF),
+            jax.ShapeDtypeStruct((hr, wide), BF),
+            jax.ShapeDtypeStruct((8, 128), F32),
+            jax.ShapeDtypeStruct((8, LO, 4 * nf), BF),
         ),
-        in_specs=[anyspace, vm, anyspace, vm, vm, vm, anyspace, anyspace, vm, vm, anyspace],
-        out_specs=(vm, vm, anyspace),
+        in_specs=[hbm, vm, hbm, vm, vm, vm, hbm, hbm, vm, vm, hbm],
+        out_specs=(hbm, vm, hbm),
         scratch_shapes=[
             V((hr + 128, wide), BF),
-            V((wide, 64), BF),
+            V((64, wide), BF),
             V((3 * HI, HI), BF),
-            V((3 * HI, 2 * LO), BF),
-            V((8, 4 * nf, LO), BF),
             V((hr + 80, 128), F32),
             V((hr + 80, 128), F32),
             V((nf, 4, 128), F32),
             V((nf, 4, 128), F32),
-            V((rows, 256), BF),
+            V((256, rows), BF),
             V((nf, 16, 256), BF),
             V((nf, 16, 256), BF),
             V((line, 128), F32),
@@ -435,12 +461,12 @@
             V((rows, line), BF),
             V((512, 256), BF),
             V((HI, HI), BF),
-            V((3 * HI, 256), BF),
+            V((768, HI), BF),
             V((8, 128), F32),
             V((rows, HI), F32),
             V((rows, 3 * HI), BF),
             V((rows, HI), BF),
-            V((3, rows + 8, 256), F32),
+            V((rows + 8, 768), F32),
             V((rows, 256), F32),
             V((rows, 512), BF),
             V((nf, 16, 256), BF),
@@ -453,42 +479,39 @@
             V((line, 128), F32),
             V((nf, 4, 128), F32),
             V((2, nf, 4, 128), F32),
-            V((8, 128), F32),
-            V((2 * nc, 8, 128), F32),
+            V((1, 128), F32),
+            V((nc, 1, 128), F32),
             V((hr + 80, 128), F32),
-            dma((6,)),
+            V((nf, 16, 256), BF),
+            V((hr, 128), F32),
+            V((3, hr, 128), F32),
+            V((hr, wide), BF),
+            V((8, LO, 4 * nf), BF),
+            dma((20,)),
         ]
         + [dma] * 14,
         compiler_params=pltpu.CompilerParams(
-            collective_id=0, has_side_effects=True, vmem_limit_bytes=48 * 1024 * 1024
+            collective_id=0, has_side_effects=True, vmem_limit_bytes=60 * 1024 * 1024
         ),
         name="exchange",
     )(
-        hid, modulation[0], head_w, clip_ids, w_in, gain_one[None], w_one.reshape(3 * HI, HI),
-        w_up.reshape(3 * HI, 2 * LO), gain_two[None], w_two, reward_grad[0],
+        hid, modulation[0], head_w.T, clip_ids, w_in, gain_one, w_one.reshape(3 * HI, HI),
+        jnp.transpose(w_up, (0, 2, 1)), gain_two, w_two, jnp.transpose(reward_grad[0], (0, 2, 1)),
     )
-    cut = 512 if wide % 512 == 0 else wide
-    grad, decoded = pl.pallas_call(
-        functools.partial(last_kernel, nf),
-        grid=(wide // cut,),
+    parts = min(4, hr // 16)
+    grad, dect = pl.pallas_call(
+        functools.partial(last_kernel, parts),
         out_shape=(
             jax.ShapeDtypeStruct((hr, wide), BF),
-            jax.ShapeDtypeStruct((8, 4 * nf, LO), BF),
+            jax.ShapeDtypeStruct((8, LO, 4 * nf), BF),
         ),
-        in_specs=[
-            pl.BlockSpec((hr, 128), lambda i: (0, 0)),
-            pl.BlockSpec((64, cut), lambda i: (0, i)),
-            pl.BlockSpec((hr, cut), lambda i: (0, i)),
-            pl.BlockSpec((nf, 16, 256), lambda i: (0, 0, 0)),
-        ],
-        out_specs=(
-            pl.BlockSpec((hr, cut), lambda i: (0, i)),
-            pl.BlockSpec((8, 4 * nf, LO), lambda i: (0, 0, 0)),
-        ),
-        compiler_params=pltpu.CompilerParams(vmem_limit_bytes=32 * 1024 * 1024),
+        in_specs=[pl.BlockSpec(memory_space=pl.ANY), vm, pl.BlockSpec(memory_space=pl.ANY)],
+        out_specs=(hbm, hbm),
+        scratch_shapes=[V((hr, wide), BF), V((hr, wide), BF), V((8, LO, 4 * nf), BF), dma((1 + 2 * parts,))],
+        compiler_params=pltpu.CompilerParams(vmem_limit_bytes=60 * 1024 * 1024),
         name="finish",
-    )(coef, wr, hid, rd)
-    return decoded[None], grad.reshape(hidden.shape)
+    )(raw, scale, dect)
+    return jnp.transpose(dect, (0, 2, 1))[None], grad.reshape(hidden.shape)
 
 
 def solution(mesh):

time: 58.2 us -> 51.1 us (0.88)
  local copies, waits for them, and re-layouts: 5.49 us -> 0 us
  Pallas kernels: 51.7 us -> 50.2 us
    unnamed x20 -> x0, local copies, waits for them, and re-layouts: 4.68 us -> none
    pallas_call x1, Pallas kernels: 48.4 us -> 47.3 us  [body(): pl.pallas_call(functools.partial(main_kernel, nf, nc, dd, count), out_sha...]
    broadcast_in_dim x1 -> x0, local copies, waits for them, and re-layouts: 0.81 us -> none  [body(): gain_one[None]]
where the time goes in v2:
time: 51.1 us; the launch traced here: 50.9 us
  Pallas kernels  50.2 us (98%)
  between operations  0.64 us (1%)
    pallas_call x1, Pallas kernels, body(): pl.pallas_call(functools.partial(main_kernel, nf, nc, dd, count), out_sha...  47.3 us
    pallas_call x1, Pallas kernels, body(): pl.pallas_call(functools.partial(last_kernel, parts), out_shape=(jax.Shap...  2.93 us

profile of v2, /device:TPU:1, one launch (start us, length us, event | category | flops | bytes accessed | tf_op | source)
XLA Modules:
  0.0 50.9 jit_solution(16018546752343772262)
XLA Ops:
  0.6 47.3 %exchange.1 = (bf16[256,2560]{1,0:T(8,128)(2,1)}, f32[8,128]{1,0:T(8,128)}, bf16[8,96,128]{2,1,0:T(8,128)(2,1)}) custom-call(bf16[256,2560]{1,0:T(8,128)(2,1)} %bitcast.12, f32[2,2560]{1,0:T(2,128)} %bitcast.17, bf16[64,2560]{1,0:T(8,128)(2,1)} %bitcast.15, s32[1,128]{1,0:T(1,128)} %ids.1, bf16[3,16,384]{2,1,0:T(8,128)(2,1)} %w_in.1, f32[384]{0:T(512)} %gain1.1, ...), custom_call_target="tpu_custom_call" | custom-call | tf_op jit(solution)/shard_map/exchange/pallas_call | solution.py:438
  47.9 2.9 %finish.1 = (bf16[256,2560]{1,0:T(8,128)(2,1)}, bf16[8,96,128]{2,1,0:T(8,128)(2,1)}) custom-call(bf16[256,2560]{1,0:T(8,128)(2,1)} %get-tuple-element.7.raw, f32[8,128]{1,0:T(8,128)} %get-tuple-element.8.scale, bf16[8,96,128]{2,1,0:T(8,128)(2,1)} %get-tuple-element.9.dect), custom_call_target="tpu_custom_call" | custom-call | tf_op jit(solution)/shard_map/finish/pallas_call | solution.py:502

commit v3 on v2

--- a/solution.py
+++ b/solution.py
@@ -57,10 +57,10 @@
 
 def main_kernel(
     nf, nc, dd, count,
-    hidden, mod, head_w, ids, w_in, gain1, w_one, w_up, gain2, w_two, reward,
+    hidden, mod_h, head_w, ids_h, w_in_h, gain1_h, w_one, w_up, gain2_h, w_two_h, reward,
     raw, scale_out, dect,
     HX, HW, W1, XS, XR, X2, RX, SRC, SR, RW, LTS, MT, MS, REP, WD, WI, WUP, G2,
-    B, AC, TR, U, UP, A2, DEC, HS, UG, JL, TG, BG, ZM, PS, X3, RXA, ZS, ZB, ST, RD, FIN, KB, RAW, DT,
+    B, AC, TR, U, UP, A2, DEC, HS, UG, JL, TG, BG, ZM, PS, X3, RXA, ZS, ZB, ST, RD, FIN, KB, RAW, DT, mod, ids, w_in, gain1, gain2, w_two, SC,
     lsem, sec_s, sec_r, lat_s, lat_r, rew_s, rew_r, dec_s, dec_r, lg_s, lg_r, sx_s, sx_r, z_s, z_r,
 ):
     sec = lax.axis_index("sec")
@@ -73,7 +73,7 @@
 
     edge = 4 * nf
     loads = [
-        [pltpu.make_async_copy(head_w, HW, lsem.at[0])],
+        [pltpu.make_async_copy(head_w, HW, lsem.at[0]), pltpu.make_async_copy(mod_h, mod, lsem.at[20])],
         [pltpu.make_async_copy(hidden, HX.at[pl.ds(0, hr)], lsem.at[1])],
         [
             pltpu.make_async_copy(
@@ -88,13 +88,19 @@
             for k in range(3) for i in range(2)
         ],
         [pltpu.make_async_copy(w_one, W1, lsem.at[4])],
+        [
+            pltpu.make_async_copy(src, dst, lsem.at[21 + i])
+            for i, (src, dst) in enumerate(
+                ((ids_h, ids), (w_in_h, w_in), (gain1_h, gain1), (gain2_h, gain2), (w_two_h, w_two))
+            )
+        ],
     ]
 
     def load(which):
         for copy in loads[which]:
             copy.wait()
 
-    for group in loads:
+    for group in loads[:2]:
         for copy in group:
             copy.start()
 
@@ -114,6 +120,9 @@
     for d in above:
         pl.semaphore_signal(barrier, inc=1, device_id=(sec, frm, d), device_id_type=MESH)
     pl.semaphore_signal(barrier, inc=1, device_id=(1 - sec, frm, clip), device_id_type=MESH)
+    for group in loads[2:]:
+        for copy in group:
+            copy.start()
 
     def to_all(src, dst, ssem, rsem):
         for d in peers:
@@ -157,6 +166,7 @@
     )
     swap.start()
 
+    load(5)
     when = iota((line, 128), 0)
     own = jnp.broadcast_to(ids[...].astype(F32), (128, line)).T
     mt1 = jnp.where((own == pltpu.roll(own, 1, 0)) & (when >= 1), 1.0, 0.0)
@@ -239,7 +249,7 @@
         AC[pl.ds(at, RB), 2 * HI : 3 * HI] = (ext[0:RB] * m2).astype(BF)
         return ext[RB:]
 
-    lax.fori_loop(0, steps, act_one, jnp.zeros((8, HI), F32))
+    lax.fori_loop(0, steps, act_one, jnp.zeros((8, HI), F32), unroll=True)
     load(4)
     TR[...] = (B[...] + nn(AC[...], W1[...])).astype(BF)
     U[pl.ds(8, rows), :] = nt(TR[...], WUP[...])
@@ -259,7 +269,7 @@
         A2[pl.ds(at, RB), 256:512] = (ext[4 : RB + 4] * m1).astype(BF)
         return ext[RB:]
 
-    lax.fori_loop(0, steps, act_two, jnp.zeros((8, 256), F32))
+    lax.fori_loop(0, steps, act_two, jnp.zeros((8, 256), F32), unroll=True)
     DEC[...] = (UP[...] + nn(A2[...], WD[...])).astype(BF).reshape(nf, 16, 256)
     to_all(DEC, RD, dec_s, dec_r)
     RD[pl.ds(frm, 1)] = DEC[pl.ds(frm, 1)]
@@ -278,7 +288,7 @@
         UG[pl.ds(at, RB), :] = (g + jnp.concatenate(back, axis=1)).astype(BF)
         return c
 
-    lax.fori_loop(0, steps, up_grad, 0)
+    lax.fori_loop(0, steps, up_grad, 0, unroll=True)
     for k in range(3):
         JL[pl.ds(0, rows), HI * k : HI * k + HI] = nn(UG[...], WUP[pl.ds(256 * k, 256), :])
 
@@ -294,7 +304,7 @@
         TG[pl.ds(at, RB), :] = gathered(at).astype(BF)
         return c
 
-    lax.fori_loop(0, steps, trunk_grad, 0)
+    lax.fori_loop(0, steps, trunk_grad, 0, unroll=True)
     JL[pl.ds(0, rows), :] = nt(TG[...], W1[...])
 
     def base_grad(b, c):
@@ -303,7 +313,7 @@
         BG[pl.ds(at, RB), :] = (TG[pl.ds(at, RB), :].astype(F32) + back).astype(BF)
         return c
 
-    lax.fori_loop(0, steps, base_grad, 0)
+    lax.fori_loop(0, steps, base_grad, 0, unroll=True)
     ZM[...] = jnp.where(mine, nt(BG[...], WI[...]), 0.0).astype(BF)
     rep_t = one_hot(iota((line, rows), 0) == iota((line, rows), 1) // 4)
     y = nn(rep_t, ZM[...])
@@ -371,7 +381,7 @@
         RAW[:, at] = (grads * tile(KB[0], 2) + tile(KB[1], 2) - h * tile(KB[2], 2)).astype(BF)
         return carry
 
-    lax.fori_loop(0, HX.shape[1] // 256, token_grad, 0)
+    lax.fori_loop(0, HX.shape[1] // 256, token_grad, 0, unroll=2)
     out_raw = pltpu.make_async_copy(RAW, raw, lsem.at[0])
     out_raw.start()
 
@@ -394,7 +404,10 @@
     z_all.wait_recv()
     total = jnp.sum(ZB[:, 0, :], axis=0, keepdims=True)[:, 66:67]
     grow = lax.rsqrt(jnp.maximum(total, 0.0) * (1.0 / count) + EPS)
-    scale_out[...] = jnp.broadcast_to(grow, (8, 128))
+    SC[...] = jnp.broadcast_to(grow, (8, 128))
+    out_scale = pltpu.make_async_copy(SC, scale_out, lsem.at[2])
+    out_scale.start()
+    out_scale.wait()
     out_raw.wait()
     out_dec.wait()
 
@@ -405,7 +418,9 @@
     z_all.wait_send()
 
 
-def last_kernel(parts, raw, scale, dect, out, decoded, got, done, dec, sems):
+def last_kernel(parts, raw, scale_h, dect, out, decoded, got, done, dec, scale, sems):
+    factor = pltpu.make_async_copy(scale_h, scale, sems.at[1 + 2 * parts])
+    factor.start()
     size = got.shape[0] // parts
     inward = pltpu.make_async_copy(dect, dec, sems.at[0])
     outward = pltpu.make_async_copy(dec, decoded, sems.at[0])
@@ -414,6 +429,7 @@
     for read in reads:
         read.start()
     inward.start()
+    factor.wait()
     writes = []
     for p, at in enumerate(spots):
         reads[p].wait()
@@ -432,7 +448,6 @@
     rows, line, hr = 16 * nf, 4 * nf, 8 * nf
     hid = hidden.reshape(hr, wide)
     hbm = pl.BlockSpec(memory_space=pltpu.HBM)
-    vm = pl.BlockSpec(memory_space=pltpu.VMEM)
     dma = pltpu.SemaphoreType.DMA
     V = pltpu.VMEM
     raw, scale, dect = pl.pallas_call(
@@ -442,8 +457,8 @@
             jax.ShapeDtypeStruct((8, 128), F32),
             jax.ShapeDtypeStruct((8, LO, 4 * nf), BF),
         ),
-        in_specs=[hbm, vm, hbm, vm, vm, vm, hbm, hbm, vm, vm, hbm],
-        out_specs=(hbm, vm, hbm),
+        in_specs=[hbm] * 11,
+        out_specs=(hbm, hbm, hbm),
         scratch_shapes=[
             V((hr + 128, wide), BF),
             V((64, wide), BF),
@@ -487,7 +502,14 @@
             V((3, hr, 128), F32),
             V((hr, wide), BF),
             V((8, LO, 4 * nf), BF),
-            dma((20,)),
+            V((2, wide), F32),
+            V((1, line), jnp.int32),
+            V((3, 16, HI), BF),
+            V((HI,), F32),
+            V((LO,), F32),
+            V((3, LO, LO), BF),
+            V((8, 128), F32),
+            dma((26,)),
         ]
         + [dma] * 14,
         compiler_params=pltpu.CompilerParams(
@@ -505,9 +527,9 @@
             jax.ShapeDtypeStruct((hr, wide), BF),
             jax.ShapeDtypeStruct((8, LO, 4 * nf), BF),
         ),
-        in_specs=[pl.BlockSpec(memory_space=pl.ANY), vm, pl.BlockSpec(memory_space=pl.ANY)],
+        in_specs=[hbm, hbm, hbm],
         out_specs=(hbm, hbm),
-        scratch_shapes=[V((hr, wide), BF), V((hr, wide), BF), V((8, LO, 4 * nf), BF), dma((1 + 2 * parts,))],
+        scratch_shapes=[V((hr, wide), BF), V((hr, wide), BF), V((8, LO, 4 * nf), BF), V((8, 128), F32), dma((2 + 2 * parts,))],
         compiler_params=pltpu.CompilerParams(vmem_limit_bytes=60 * 1024 * 1024),
         name="finish",
     )(raw, scale, dect)

time: 51.1 us -> 45.9 us (0.90)
  Pallas kernels: 50.2 us -> 45.1 us
    pallas_call x1, Pallas kernels: 47.3 us -> 42.9 us  [body(): pl.pallas_call(functools.partial(main_kernel, nf, nc, dd, count), out_sha...]
    pallas_call x1, Pallas kernels: 2.93 us -> 2.27 us  [body(): pl.pallas_call(functools.partial(last_kernel, parts), out_shape=(jax.Shap...]
where the time goes in v3:
time: 45.9 us; the launch traced here: 45.8 us
  Pallas kernels  45.1 us (98%)
  between operations  0.64 us (1%)
    pallas_call x1, Pallas kernels, body(): pl.pallas_call(functools.partial(main_kernel, nf, nc, dd, count), out_sha...  42.9 us
    pallas_call x1, Pallas kernels, body(): pl.pallas_call(functools.partial(last_kernel, parts), out_shape=(jax.Shap...  2.27 us

profile of v3, /device:TPU:1, one launch (start us, length us, event | category | flops | bytes accessed | tf_op | source)
XLA Modules:
  0.0 45.8 jit_solution(10482257584119477644)
XLA Ops:
  0.6 42.9 %exchange.1 = (bf16[256,2560]{1,0:T(8,128)(2,1)}, f32[8,128]{1,0:T(8,128)}, bf16[8,96,128]{2,1,0:T(8,128)(2,1)}) custom-call(bf16[256,2560]{1,0:T(8,128)(2,1)} %bitcast.12, f32[2,2560]{1,0:T(2,128)} %bitcast.17, bf16[64,2560]{1,0:T(8,128)(2,1)} %bitcast.15, s32[1,128]{1,0:T(1,128)} %ids_h.1, bf16[3,16,384]{2,1,0:T(8,128)(2,1)} %w_in_h.1, f32[384]{0:T(512)} %gain1_h.1, ...), custom_call_target="tpu_custom_call" | custom-call | tf_op jit(solution)/shard_map/exchange/pallas_call | solution.py:453
  43.5 2.3 %finish.1 = (bf16[256,2560]{1,0:T(8,128)(2,1)}, bf16[8,96,128]{2,1,0:T(8,128)(2,1)}) custom-call(bf16[256,2560]{1,0:T(8,128)(2,1)} %get-tuple-element.7.raw, f32[8,128]{1,0:T(8,128)} %get-tuple-element.8.scale_h, bf16[8,96,128]{2,1,0:T(8,128)(2,1)} %get-tuple-element.9.dect), custom_call_target="tpu_custom_call" | custom-call | tf_op jit(solution)/shard_map/finish/pallas_call | solution.py:524

commit v4 on v3

--- a/solution.py
+++ b/solution.py
@@ -107,10 +107,14 @@
     nx = 4
     ny = nf // nx
     yy, xx = frm // nx, lax.rem(frm, nx)
-    far = sorted(
-        ((min(dy, ny - dy) + min(dx, nx - dx), dy, dx) for dy in range(ny) for dx in range(nx) if dy or dx),
-        reverse=True,
-    )
+    ways = [(min(dy, ny - dy) + min(dx, nx - dx), dy, dx) for dy in range(ny) for dx in range(nx) if dy or dx]
+    seen = {}
+    far = []
+    for hop, dy, dx in sorted(ways, reverse=True):
+        side = (hop, 2 * dy > ny)
+        seen[side] = seen.get(side, 0) + 1
+        far.append((-hop, seen[side], dy, dx))
+    far = [(-hop, dy, dx) for hop, _, dy, dx in sorted(far)]
     peers = [lax.rem(yy + dy, ny) * nx + lax.rem(xx + dx, nx) for _, dy, dx in far]
     above = [lax.rem(clip + dz, nc) for dz in sorted(range(1, nc), key=lambda dz: -min(dz, nc - dz))]
 
@@ -124,8 +128,8 @@
         for copy in group:
             copy.start()
 
-    def to_all(src, dst, ssem, rsem):
-        for d in peers:
+    def to_all(src, dst, ssem, rsem, some=slice(None)):
+        for d in peers[some]:
             pltpu.make_async_remote_copy(
                 src_ref=src.at[d], dst_ref=dst.at[frm], send_sem=ssem, recv_sem=rsem,
                 device_id=(sec, d, clip), device_id_type=MESH,
@@ -271,7 +275,7 @@
 
     lax.fori_loop(0, steps, act_two, jnp.zeros((8, 256), F32), unroll=True)
     DEC[...] = (UP[...] + nn(A2[...], WD[...])).astype(BF).reshape(nf, 16, 256)
-    to_all(DEC, RD, dec_s, dec_r)
+    to_all(DEC, RD, dec_s, dec_r, slice(0, 16))
     RD[pl.ds(frm, 1)] = DEC[pl.ds(frm, 1)]
 
     all_of(SR, RW, rew_s, rew_r).wait_recv()
@@ -350,6 +354,7 @@
         device_id=(1 - sec, frm, clip), device_id_type=MESH,
     )
     trade.start()
+    to_all(DEC, RD, dec_s, dec_r, slice(16, None))
     trade.wait()
     everyone = jnp.sum(RXA[0, :, 0, :] + RXA[1, :, 0, :], axis=0, keepdims=True)
     ZS[...] = everyone

time: 45.9 us -> 44.8 us (0.976)
  Pallas kernels: 45.1 us -> 44 us
    pallas_call x1, Pallas kernels: 42.9 us -> 41.7 us  [body(): pl.pallas_call(functools.partial(main_kernel, nf, nc, dd, count), out_sha...]
where the time goes in v4:
time: 44.8 us; the launch traced here: 44.7 us
  Pallas kernels  44 us (98%)
  between operations  0.64 us (1%)
    pallas_call x1, Pallas kernels, body(): pl.pallas_call(functools.partial(main_kernel, nf, nc, dd, count), out_sha...  41.7 us
    pallas_call x1, Pallas kernels, body(): pl.pallas_call(functools.partial(last_kernel, parts), out_shape=(jax.Shap...  2.27 us

profile of v4, /device:TPU:1, one launch (start us, length us, event | category | flops | bytes accessed | tf_op | source)
XLA Modules:
  0.0 44.7 jit_solution(18102662027685834023)
XLA Ops:
  0.6 41.7 %exchange.1 = (bf16[256,2560]{1,0:T(8,128)(2,1)}, f32[8,128]{1,0:T(8,128)}, bf16[8,96,128]{2,1,0:T(8,128)(2,1)}) custom-call(bf16[256,2560]{1,0:T(8,128)(2,1)} %bitcast.12, f32[2,2560]{1,0:T(2,128)} %bitcast.17, bf16[64,2560]{1,0:T(8,128)(2,1)} %bitcast.15, s32[1,128]{1,0:T(1,128)} %ids_h.1, bf16[3,16,384]{2,1,0:T(8,128)(2,1)} %w_in_h.1, f32[384]{0:T(512)} %gain1_h.1, ...), custom_call_target="tpu_custom_call" | custom-call | tf_op jit(solution)/shard_map/exchange/pallas_call | solution.py:458
  42.4 2.3 %finish.1 = (bf16[256,2560]{1,0:T(8,128)(2,1)}, bf16[8,96,128]{2,1,0:T(8,128)(2,1)}) custom-call(bf16[256,2560]{1,0:T(8,128)(2,1)} %get-tuple-element.7.raw, f32[8,128]{1,0:T(8,128)} %get-tuple-element.8.scale_h, bf16[8,96,128]{2,1,0:T(8,128)(2,1)} %get-tuple-element.9.dect), custom_call_target="tpu_custom_call" | custom-call | tf_op jit(solution)/shard_map/finish/pallas_call | solution.py:529

commit v5 on v4

--- a/solution.py
+++ b/solution.py
@@ -211,20 +211,22 @@
     load(3)
 
     swap.wait()
-    ST[...] = XS[...] + XR[...]
+    ST[pl.ds(hr, 80), :] = XS[pl.ds(hr, 80), :] + XR[pl.ds(hr, 80), :]
     consts = ST[pl.ds(hr + 64, 16), :]
     col_sum = consts[0:1, :]
     sw = consts[8:9, :]
-    stats = ST[pl.ds(0, hr), :]
-    mean = stats[:, 64:65] * (1.0 / dd)
-    inv = lax.rsqrt(stats[:, 80:81] * (1.0 / dd) - mean * mean + EPS)
+    own_half = sec * nf
     hl = iota((hr, 128), 1)
-    pay = jnp.where(hl < 64, inv * (stats - mean * col_sum), jnp.where(hl == 64, inv, 0.0))
-    XS[pl.ds(0, hr), :] = pay
+    nl = iota((nf, 128), 1)
     for j in range(4):
-        X2[:, j, :] = XS[pl.ds(pl.multiple_of(j * 2 * nf + sec * nf, 8) if nf % 8 == 0 else j * 2 * nf + sec * nf, nf), :]
+        at = pl.ds(pl.multiple_of(j * 2 * nf + own_half, 8) if nf % 8 == 0 else j * 2 * nf + own_half, nf)
+        stats = XS[at, :] + XR[at, :]
+        mean = stats[:, 64:65] * (1.0 / dd)
+        inv = lax.rsqrt(stats[:, 80:81] * (1.0 / dd) - mean * mean + EPS)
+        X2[:, j, :] = jnp.where(nl < 64, inv * (stats - mean * col_sum), jnp.where(nl == 64, inv, 0.0))
     to_all(X2, RX, lat_s, lat_r)
     to_all(SR, RW, rew_s, rew_r)
+    ST[pl.ds(0, hr), :] = XS[pl.ds(0, hr), :] + XR[pl.ds(0, hr), :]
     RX[pl.ds(frm, 1)] = X2[pl.ds(frm, 1)]
     RW[pl.ds(frm, 1)] = SR[pl.ds(frm, 1)]
     all_of(X2, RX, lat_s, lat_r).wait_recv()
@@ -275,7 +277,7 @@
 
     lax.fori_loop(0, steps, act_two, jnp.zeros((8, 256), F32), unroll=True)
     DEC[...] = (UP[...] + nn(A2[...], WD[...])).astype(BF).reshape(nf, 16, 256)
-    to_all(DEC, RD, dec_s, dec_r, slice(0, 16))
+    to_all(DEC, RD, dec_s, dec_r, slice(0, 20))
     RD[pl.ds(frm, 1)] = DEC[pl.ds(frm, 1)]
 
     all_of(SR, RW, rew_s, rew_r).wait_recv()
@@ -354,7 +356,7 @@
         device_id=(1 - sec, frm, clip), device_id_type=MESH,
     )
     trade.start()
-    to_all(DEC, RD, dec_s, dec_r, slice(16, None))
+    to_all(DEC, RD, dec_s, dec_r, slice(20, None))
     trade.wait()
     everyone = jnp.sum(RXA[0, :, 0, :] + RXA[1, :, 0, :], axis=0, keepdims=True)
     ZS[...] = everyone

time: 44.8 us -> 45 us (level)
  no operation moved by 1% of the time
where the time goes in v5:
time: 45 us; the launch traced here: 44.8 us
  Pallas kernels  44.2 us (98%)
  between operations  0.64 us (1%)
    pallas_call x1, Pallas kernels, body(): pl.pallas_call(functools.partial(main_kernel, nf, nc, dd, count), out_sha...  41.9 us
    pallas_call x1, Pallas kernels, body(): pl.pallas_call(functools.partial(last_kernel, parts), out_shape=(jax.Shap...  2.27 us

profile of v5, /device:TPU:1, one launch (start us, length us, event | category | flops | bytes accessed | tf_op | source)
XLA Modules:
  0.0 44.8 jit_solution(10511388196731478816)
XLA Ops:
  0.6 41.9 %exchange.1 = (bf16[256,2560]{1,0:T(8,128)(2,1)}, f32[8,128]{1,0:T(8,128)}, bf16[8,96,128]{2,1,0:T(8,128)(2,1)}) custom-call(bf16[256,2560]{1,0:T(8,128)(2,1)} %bitcast.12, f32[2,2560]{1,0:T(2,128)} %bitcast.17, bf16[64,2560]{1,0:T(8,128)(2,1)} %bitcast.15, s32[1,128]{1,0:T(1,128)} %ids_h.1, bf16[3,16,384]{2,1,0:T(8,128)(2,1)} %w_in_h.1, f32[384]{0:T(512)} %gain1_h.1, ...), custom_call_target="tpu_custom_call" | custom-call | tf_op jit(solution)/shard_map/exchange/pallas_call | solution.py:460
  42.5 2.3 %finish.1 = (bf16[256,2560]{1,0:T(8,128)(2,1)}, bf16[8,96,128]{2,1,0:T(8,128)(2,1)}) custom-call(bf16[256,2560]{1,0:T(8,128)(2,1)} %get-tuple-element.7.raw, f32[8,128]{1,0:T(8,128)} %get-tuple-element.8.scale_h, bf16[8,96,128]{2,1,0:T(8,128)(2,1)} %get-tuple-element.9.dect), custom_call_target="tpu_custom_call" | custom-call | tf_op jit(solution)/shard_map/finish/pallas_call | solution.py:531
